TPU v7x, 32 devices: a whole 2x2x4 slice. The times are simulated.
32 devices in a mesh: dp: 4 (over z), tm: 4 (over y, core), height: 2 (over x).
Axes of the slice: x: 2, y: 2, z: 4, core: 2. Of those that a mesh axis runs over, the one named last changes fastest.
Arguments:
- clip_inputs: bfloat16 [4, 8, 4, 16, 512], P('dp', 'tm', 'height'), may hold values from -6 to 6
- conv_in_weight: bfloat16 [13824, 512], P(('tm', 'height'), 'dp'), may hold values from -0.0546875 to 0.0546875
- group_gain: bfloat16 [512], P('dp'), may hold values from 0.099609375 to 1.8984375
- group_bias: bfloat16 [512], P('dp'), may hold values from -3 to 3
- conv_out_weight: bfloat16 [27, 512, 16], P(None, 'dp'), may hold values from -0.109375 to 0.109375
- out_bias: float32 [16], replicated, may hold values from -3 to 3
- patch_weight: bfloat16 [64, 3072], replicated, may hold values from -1.5 to 1.5
- patch_bias: bfloat16 [3072], replicated, may hold values from -3 to 3
- qkv_weight: bfloat16 [3072, 3072], P(('tm', 'height'), 'dp'), may hold values from -0.109375 to 0.109375
- qkv_bias: bfloat16 [3072], P('dp'), may hold values from -3 to 3
- q_gain: bfloat16 [128], replicated, may hold values from 0.099609375 to 1.8984375
- k_gain: bfloat16 [128], replicated, may hold values from 0.099609375 to 1.8984375
- frame_pos: int32 [8], P('tm'), may hold values from 0 to 63
- row_pos: int32 [2], P('height'), may hold values from 0 to 127
Outputs:
- latents: float32 [4, 8, 4, 256], P('dp', 'tm', 'height')
- queries: bfloat16 [4, 8, 2, 8, 1024], P(None, 'tm', 'height', None, 'dp')
- keys: bfloat16 [4, 8, 2, 8, 1024], P(None, 'tm', 'height', None, 'dp')
- values: bfloat16 [4, 8, 2, 8, 1024], P(None, 'tm', 'height', None, 'dp')
All inputs are finite; a program needn't handle non-finite values.
Results may differ from a plain program's by a relative error of at most 0.01.
Values may be sent and summed in bfloat16 or wider, within the bound.
No kernel may reach another device: no remote copies, remote signals or barrier semaphores. Data moves between devices by JAX's collectives and lax.ppermute only.
A program may use at most 64 MiB of HBM per device.

v0:
```python
import functools

import jax
import jax.numpy as jnp
import numpy as np
from jax import lax
from jax.experimental import pallas as pl
from jax.experimental.pallas import tpu as pltpu
from jax.sharding import PartitionSpec as P

HD = 128
GROUPS = 32
TAPS = 27


norm_eps = 1e-06
latent_scale = 0.476986
rope_base = 256.0
time_dims = 16
row_dims = 56


def from_behind(value, axis, steps):
    count = lax.axis_size(axis)
    first, last = (max(0, -steps), min(count, count - steps))
    return lax.ppermute(value, axis, [(source, source + steps) for source in range(first, last)])


def padded_2(block, sides, width):
    for axis, dim in sides:
        count = lax.axis_size(axis)
        forward = [(i, i + 1) for i in range(count - 1)]
        backward = [(target, source) for source, target in forward]
        low = lax.ppermute(
            lax.slice_in_dim(block, block.shape[dim] - width, None, axis=dim), axis, forward
        )
        high = lax.ppermute(lax.slice_in_dim(block, 0, width, axis=dim), axis, backward)
        block = jnp.concatenate([low, block, high], axis=dim)
    return block


def repeat_first(block):
    return jnp.concatenate([block[:, :1], block[:, :1]], axis=1)


def time_join(block, earlier):
    start = jnp.where(lax.axis_index("tm") == 0, repeat_first(block), earlier)
    return jnp.concatenate([start, block], axis=1)


def rows_finish(grown):
    place = lax.axis_index("height")
    top = jnp.where(place == 0, grown[:, :, 1:2], grown[:, :, :1])
    bottom = jnp.where(place == lax.axis_size("height") - 1, grown[:, :, -2:-1], grown[:, :, -1:])
    inner = jnp.concatenate([top, grown[:, :, 1:-1], bottom], axis=2)
    return jnp.pad(inner, ((0, 0), (0, 0), (0, 0), (1, 1), (0, 0)), mode="edge")


def edges_before(block):
    earlier = from_behind(block, "tm", 1)
    longer = time_join(block, earlier)
    return rows_finish(padded_2(longer, (("height", 2),), 1))


def edges_norm(block):
    earlier = from_behind(block, "tm", 1)
    longer = time_join(block, earlier)
    return rows_finish(padded_2(longer, (("height", 2),), 1))


def convolve(padded, weight):
    clips = padded.shape[0]
    frames = padded.shape[1] - 2
    rows = padded.shape[2] - 2
    cols = padded.shape[3] - 2
    total = jnp.zeros((clips * frames * rows * cols, weight.shape[2]), jnp.float32)
    for shift_t in range(3):
        for shift_r in range(3):
            for shift_c in range(3):
                window = padded[
                    :,
                    shift_t : shift_t + frames,
                    shift_r : shift_r + rows,
                    shift_c : shift_c + cols,
                ]
                window = window.reshape(-1, padded.shape[4])
                total = total + jnp.dot(
                    window,
                    weight[9 * shift_t + 3 * shift_r + shift_c],
                    preferred_element_type=jnp.float32,
                )
    return total.reshape(clips, frames, rows, cols, weight.shape[2])


def section_freqs(dims):
    return jnp.power(rope_base, -jnp.arange(0, dims, 2, dtype=jnp.float32) / dims)


def rope_angles(tpos, hpos, width):
    frames = tpos.shape[0]
    rows = hpos.shape[0]
    cols = jnp.arange(width, dtype=jnp.float32)
    part_t = tpos[:, None, None, None] * section_freqs(time_dims)
    part_h = hpos[None, :, None, None] * section_freqs(row_dims)
    part_w = cols[None, None, :, None] * section_freqs(row_dims)
    shape = (frames, rows, width)
    return jnp.concatenate(
        [
            jnp.broadcast_to(part_t, shape + (time_dims // 2,)),
            jnp.broadcast_to(part_h, shape + (row_dims // 2,)),
            jnp.broadcast_to(part_w, shape + (row_dims // 2,)),
        ],
        axis=-1,
    )


def rotate(vectors, angles):
    pairs = vectors.reshape(vectors.shape[:-1] + (vectors.shape[-1] // 2, 2))
    first = pairs[..., 0]
    second = pairs[..., 1]
    cosine = jnp.cos(angles)[..., None, :]
    sine = jnp.sin(angles)[..., None, :]
    turned = jnp.stack([first * cosine - second * sine, first * sine + second * cosine], axis=-1)
    return turned.reshape(vectors.shape)


def rms_scale(vectors, gain):
    return (
        vectors
        * lax.rsqrt(jnp.mean(vectors * vectors, axis=-1, keepdims=True) + norm_eps)
        * gain.astype(jnp.float32)
    )


def shards(
    clip_inputs,
    conv_in_weight,
    group_gain,
    group_bias,
    conv_out_weight,
    out_bias,
    patch_weight,
    patch_bias,
    qkv_weight,
    qkv_bias,
    q_gain,
    k_gain,
    frame_pos,
    row_pos,
):
    channels = clip_inputs.shape[4]
    frames = clip_inputs.shape[1]
    rows = clip_inputs.shape[2]
    cols = clip_inputs.shape[3]
    padded = lax.all_gather(edges_before(clip_inputs), "dp", axis=0, tiled=True)
    clips = padded.shape[0]
    weight_in = lax.all_gather(conv_in_weight, ("tm", "height"), axis=0, tiled=True).reshape(
        TAPS, channels, -1
    )
    hidden = convolve(padded, weight_in)
    block_width = hidden.shape[4]
    group_width = channels // GROUPS
    local_groups = block_width // group_width
    grouped = hidden.reshape(clips, -1, local_groups, group_width)
    sums_local = jnp.sum(grouped, axis=(1, 3))
    squares_local = jnp.sum(grouped * grouped, axis=(1, 3))
    sums_all, squares_all = lax.psum((sums_local, squares_local), ("tm", "height"))
    count = float(
        frames * lax.axis_size("tm") * rows * lax.axis_size("height") * cols * group_width
    )
    mean = sums_all / count
    var = squares_all / count - mean * mean
    scaled = (grouped - mean[:, None, :, None]) * lax.rsqrt(var + norm_eps)[:, None, :, None]
    scaled = scaled.reshape(hidden.shape) * group_gain.astype(jnp.float32) + group_bias.astype(
        jnp.float32
    )
    normed = jax.nn.silu(scaled).astype(jnp.bfloat16)
    partial_latent = convolve(edges_norm(normed), conv_out_weight)
    own_sum = lax.psum_scatter(partial_latent, "dp", scatter_dimension=0, tiled=True)
    own_latent = (own_sum + out_bias) * latent_scale
    every_latent = lax.all_gather(own_latent.astype(jnp.bfloat16), "dp", axis=0, tiled=True)
    latent_dims = every_latent.shape[4]
    latents = own_latent.reshape(1, frames, rows, cols * latent_dims)
    tok_rows = rows // 2
    tok_cols = cols // 2
    patches = every_latent.reshape(clips, frames, tok_rows, 2, tok_cols, 2, latent_dims)
    patches = patches.transpose(0, 1, 2, 4, 3, 5, 6).reshape(-1, 4 * latent_dims)
    embedded = (
        jnp.dot(patches, patch_weight, preferred_element_type=jnp.float32)
        + patch_bias.astype(jnp.float32)
    ).astype(jnp.bfloat16)
    projected = jnp.dot(
        embedded,
        lax.all_gather(qkv_weight, ("tm", "height"), axis=0, tiled=True),
        preferred_element_type=jnp.float32,
    )
    projected = projected + qkv_bias.astype(jnp.float32)
    local_heads = qkv_weight.shape[1] // (3 * HD)
    projected = projected.reshape(clips, frames, tok_rows, tok_cols, local_heads, 3, HD)
    angles = rope_angles(frame_pos.astype(jnp.float32), row_pos.astype(jnp.float32), tok_cols)
    query = rotate(rms_scale(projected[..., 0, :], q_gain), angles)
    key = rotate(rms_scale(projected[..., 1, :], k_gain), angles)
    value = projected[..., 2, :]
    merged = (clips, frames, tok_rows, tok_cols, local_heads * HD)
    return (
        latents,
        query.reshape(merged).astype(jnp.bfloat16),
        key.reshape(merged).astype(jnp.bfloat16),
        value.reshape(merged).astype(jnp.bfloat16),
    )


LANES = 128
TILE = 16
GROUP = 16


def one_group_each(mesh, clip_inputs, conv_in_weight, conv_out_weight, qkv_weight):
    plane = mesh.shape["tm"] * mesh.shape["height"]
    return (
        clip_inputs.shape[:4] == (1, 2, 2, 16)
        and mesh.shape["height"] == 2
        and mesh.shape["tm"] == 4
        and mesh.shape["dp"] == 4
        and conv_in_weight.shape[1] == plane * GROUP
        and clip_inputs.shape[4] == GROUP * GROUPS
        and conv_out_weight.shape[2] == TILE
        and qkv_weight.shape[1] == 6 * HD
    )


def lane_shifts(lane):
    col = lane % 16
    row = lane // 16 % 2
    half = lane // 64

    def cols(left, mid, right):
        left = jnp.where(col == 0, left, pltpu.roll(left, 1, 1))
        right = jnp.where(col == 15, right, pltpu.roll(right, LANES - 1, 1))
        return mid + left + right

    def rows(up, mid, down):
        up = jnp.where(
            row == 1, pltpu.roll(up, 16, 1), jnp.where(half == 1, pltpu.roll(up, 48, 1), up)
        )
        down = jnp.where(
            row == 0,
            pltpu.roll(down, LANES - 16, 1),
            jnp.where(half == 0, pltpu.roll(down, LANES - 48, 1), down),
        )
        return mid + up + down

    return cols, rows


def tap_sums(source, tiles):
    lane = lax.broadcasted_iota(jnp.int32, (TILE, LANES), 1)
    second = lane // 32 % 2 == 1
    cols, rows = lane_shifts(lane)
    sums = []
    before = None
    for tile in range(tiles):

        def part(tap):
            return source(tap, slice(tile * LANES, (tile + 1) * LANES))

        oldest, older, now = (
            rows(*(cols(*(part(9 * i + 3 * j + l) for l in range(3))) for j in range(3)))
            for i in range(3)
        )
        turned = pltpu.roll(older, 32, 1)
        if before is None:
            start = jnp.where(second, pltpu.roll(oldest, 32, 1), oldest)
            total = now + jnp.where(second, turned, older) + start
        else:
            total = now + jnp.where(second, turned, pltpu.roll(before[1], 96, 1)) + before[0]
        before = (oldest, older)
        sums.append(total)
    return sums


def pack_kernel(
    freq_hbm, w_hbm, qkv_hbm, patch_hbm, patch_bias_hbm, gain_hbm, bias_hbm, out_bias_hbm,
    qkv_bias_hbm, q_hbm, k_hbm, frame_hbm,
    own_hbm, side_hbm, high_hbm, far_hbm, scale_hbm, table_hbm,
    w_ref, qkv_ref, patch_ref, patch_bias_ref, gain_v, bias_v, out_bias_v, qkv_bias_v, q_v, k_v,
    frame_v, freq_ref, rows_ref, turned_ref, merged_ref, out_ref, lines_ref, scale_ref, table_ref, sems,
):
    _, channels, width = out_ref.shape
    depth = w_ref.shape[0]
    rows = qkv_ref.shape[0]
    side = lax.axis_index("height")
    high = lax.axis_index("tm") // 2
    place = lax.axis_index("tm") * 2 + side
    at = pl.ds(pl.multiple_of(place * rows, LANES), rows)
    pairs = (
        (w_hbm, w_ref),
        (qkv_hbm, qkv_ref),
        (patch_hbm.at[:, at], patch_ref),
        (patch_bias_hbm, patch_bias_ref),
        (gain_hbm, gain_v),
        (bias_hbm, bias_v),
        (out_bias_hbm, out_bias_v),
        (qkv_bias_hbm, qkv_bias_v),
        (q_hbm, q_v),
        (k_hbm, k_v),
        (frame_hbm, frame_v),
        (freq_hbm, freq_ref),
    )
    loads = [
        pltpu.make_async_copy(source, to, sems.at[index])
        for index, (source, to) in enumerate(pairs)
    ]
    for load in loads:
        load.start()
    whole = depth // LANES * LANES
    loads[0].wait()
    turned_ref[...] = w_ref[...].T
    for load in loads[1:4]:
        load.wait()
    merged_ref[...] = jnp.dot(patch_ref[...], qkv_ref[...], preferred_element_type=jnp.float32)
    stores = []
    own_main = own_hbm.at[:, :width]
    for flip, out_hbm in ((1, side_hbm), (2, high_hbm), (3, far_hbm), (0, own_main)):
        first = pl.multiple_of((high ^ (flip // 2)) * channels, channels)
        out_ref[flip, :, :whole] = turned_ref[pl.ds(first, channels), :whole]
        lower = turned_ref[pl.ds(first, channels), whole:]
        chip = (2 * high + side) ^ flip
        tail, upper = [], []
        for half in range(2):
            mine = merged_ref[pl.ds(pl.multiple_of(chip * 16 + half * 8, 8), 8)]
            mine = [mine[:, q * LANES : (q + 1) * LANES] for q in range(6)]
            tail += mine[:4]
            upper += [pltpu.roll(mine[4], 64, 1), mine[4], pltpu.roll(mine[5], 64, 1), mine[5]]
        upper = jnp.concatenate(upper, axis=0)[:, 64:].astype(jnp.bfloat16)
        out_ref[flip, :, whole : whole + LANES] = jnp.concatenate([lower, upper], axis=1)
        out_ref[flip, :, whole + LANES :] = jnp.concatenate(tail, axis=0).astype(jnp.bfloat16)
        stores.append(pltpu.make_async_copy(out_ref.at[flip], out_hbm, sems.at[13 + flip]))
        stores[-1].start()
    rows_ref[...] = patch_bias_ref[...].astype(jnp.float32).reshape(rows_ref.shape)
    count = rows // LANES
    bias = [rows_ref[pl.ds(count * place + part, 1), :] for part in range(count)]
    bias = jnp.broadcast_to(jnp.concatenate(bias, axis=1), (8, rows)).astype(jnp.bfloat16)
    bias = jnp.dot(bias, qkv_ref[...], preferred_element_type=jnp.float32)
    line = lax.broadcasted_iota(jnp.int32, (8, LANES), 0)
    lines = jnp.zeros((8, LANES), jnp.float32)
    for part in range(bias.shape[1] // LANES):
        lines = jnp.where(line == part, bias[:, part * LANES : (part + 1) * LANES], lines)
    lines_ref[...] = jnp.concatenate([lines, jnp.zeros_like(lines)], axis=0).astype(jnp.bfloat16)
    stores.append(
        pltpu.make_async_copy(lines_ref, own_hbm.at[:16, width : width + LANES], sems.at[17])
    )
    stores[-1].start()
    for load in loads[4:]:
        load.wait()
    fill_tables(
        frame_v, freq_ref, gain_v, bias_v, out_bias_v, qkv_bias_v, q_v, k_v,
        scale_ref, table_ref,
    )
    for index, (source, to) in enumerate(((scale_ref, scale_hbm), (table_ref, table_hbm))):
        stores.append(pltpu.make_async_copy(source, to, sems.at[18 + index]))
        stores[-1].start()
    for store in stores:
        store.wait()


def column(row_ref, first, size):
    length = row_ref.shape[0]
    row = row_ref[...].astype(jnp.float32).reshape(1, length)
    line = lax.broadcasted_iota(jnp.int32, (size, length), 0)
    lane = lax.broadcasted_iota(jnp.int32, (size, length), 1)
    picked = jnp.where(lane == line + first, jnp.broadcast_to(row, (size, length)), 0.0)
    return jnp.sum(picked, axis=1, keepdims=True)


def fill_tables(
    frame_ref, freq_ref, gain_v, bias_v, out_bias_v, qkv_v, q_v, k_v,
    scale_ref, table_ref,
):
    shape = (TILE, LANES)
    line = lax.broadcasted_iota(jnp.int32, shape, 0)
    lane = lax.broadcasted_iota(jnp.int32, shape, 1)
    frames = frame_ref[...].astype(jnp.float32).reshape(1, 2)
    one, two = (jnp.broadcast_to(frames[:, part : part + 1], shape) for part in range(2))
    frame = jnp.where(line // 8 == 0, one, two)
    spot = jnp.where(lane < 72, 1.0, (line % 8).astype(jnp.float32))
    table_ref[:16] = jnp.where(lane < 16, frame, spot) * freq_ref[...]
    table_ref[16:32] = jnp.zeros(shape, jnp.float32)
    first = lax.axis_index("tm") // 2 * (4 * GROUP)
    scale_ref[:, 0:1] = column(gain_v, first, 4 * GROUP)
    scale_ref[:, 1:2] = column(bias_v, first, 4 * GROUP)
    table_ref[32:48] = jnp.broadcast_to(column(out_bias_v, 0, TILE), shape)
    table_ref[48:49] = q_v[...].astype(jnp.float32).reshape(1, HD)
    table_ref[49:50] = k_v[...].astype(jnp.float32).reshape(1, HD)
    table_ref[50:56] = qkv_v[...].astype(jnp.float32).reshape(6, LANES)


def arrange_kernel(*refs):
    pieces, (own_ref, keep_ref, send_ref, all_ref) = refs[:4], refs[4:]
    side = lax.axis_index("height")
    layer = lax.axis_index("dp")
    for step, piece in zip(reversed(range(4)), pieces):
        all_ref[(layer + 4 - step) % 4] = piece[...]

    @pl.when(layer % 2 == lax.axis_index("tm") % 2)
    def _():
        all_ref[layer] = own_ref[...]

    for core in range(2):
        keep_ref[core] = all_ref[2 * side + core]
        send_ref[core] = all_ref[2 - 2 * side + core]


def core_taps(core):
    quarter = TAPS / 4
    taps = []
    for tm in (core, core + 2):
        taps += range(int(quarter * tm), min(TAPS, -int(-quarter * (tm + 1) // 1)))
    return taps


def join_kernel(own_ref, side_ref, high_ref, far_ref, wt_ref, all_ref):
    channels, width = side_ref.shape
    inner = wt_ref.shape[1]
    depth = TAPS * inner // 8
    here = lax.axis_index("tm") // 2 * 2 + lax.axis_index("height")
    for flip, ref in enumerate((own_ref, side_ref, high_ref, far_ref)):
        all_ref[here ^ flip] = ref[:, :width]

    def assemble(core):
        for index, tap in enumerate(core_taps(core)):
            rows = slice(index * channels, (index + 1) * channels)
            start, end = tap * inner, (tap + 1) * inner
            while start < end:
                source = start // depth
                stop = min(end, (source + 1) * depth)
                to = slice(start - tap * inner, stop - tap * inner)
                if source // 2 % 2 == core:
                    chip = source // 4 * 2 + source % 2
                    first = start - source * depth
                    wt_ref[rows, to] = all_ref[chip, :, first : first + stop - start]
                else:
                    wt_ref[rows, to] = jnp.zeros((channels, stop - start), jnp.bfloat16)
                start = stop

    core = lax.axis_index("tm") % 2
    pl.when(core == 0)(functools.partial(assemble, 0))
    pl.when(core == 1)(functools.partial(assemble, 1))
    total = sum(all_ref[chip, :, width - 2 * LANES :].astype(jnp.float32) for chip in range(4))
    low = lax.broadcasted_iota(jnp.int32, (8, LANES), 1) < 64
    empty = jnp.zeros((8, LANES), jnp.float32)
    wide, narrow = [], []
    for half in range(2):
        top = 32 * half
        wide.append([total[top + 8 * q : top + 8 * q + 8, LANES:] for q in range(4)])
        some = []
        for q in range(2):
            one = total[top + 16 * q : top + 16 * q + 8, :LANES]
            two = total[top + 16 * q + 8 : top + 16 * q + 16, :LANES]
            some.append(jnp.where(low, pltpu.roll(one, 64, 1), two))
        lines = own_ref[:16, width:].astype(jnp.float32)[8 * half : 8 * half + 8]
        narrow.append(some + [lines, empty])
    share = jnp.concatenate([jnp.concatenate(row, axis=1) for row in wide + narrow], axis=0)
    wt_ref[wt_ref.shape[0] - 32 :] = share.astype(jnp.bfloat16)


def place_kernel(*refs):
    pieces, x_ref = refs[:4], refs[4]
    place = lax.axis_index("tm") // 2 * 4 + lax.axis_index("height")
    for flip, piece in zip((0, 1, 4, 5), pieces):
        for core in range(2):
            x_ref[(place ^ flip) + 2 * core] = piece[core]


def tap_parts(y_ref, group, channels):
    held = [core_taps(core) for core in range(2)]

    def part(tap, lanes):
        found = []
        for core in range(2):
            if tap in held[core]:
                at = held[core].index(tap) * channels + group * GROUP
                found.append(y_ref[core, at : at + GROUP, lanes])
        return sum(found[1:], found[0])

    return part


def conv_kernel(
    x_ref, wt_ref, pair_ref, scale_ref, w2_ref, out_ref, y_ref
):
    channels = 4 * GROUP
    tiles = x_ref.shape[0] // 2
    count = float(tiles * LANES * GROUP)
    core = lax.axis_index("tm") % 2
    height = y_ref.shape[1]
    x = x_ref[...].reshape(tiles * LANES, x_ref.shape[2])
    for ref, at in ((wt_ref, core), (pair_ref, 1 - core)):
        y_ref[at] = lax.dot_general(
            ref[:height], x, (((1,), (1,)), ((), ())), preferred_element_type=jnp.float32
        )
    normed = []
    for group in range(4):
        hidden = tap_sums(tap_parts(y_ref, group, channels), tiles)
        at = slice(group * GROUP, (group + 1) * GROUP)
        mean = jnp.sum(sum(hidden), keepdims=True) / count
        square = jnp.sum(sum(part * part for part in hidden), keepdims=True) / count
        scale = lax.rsqrt(square - mean * mean + norm_eps)
        parts = []
        for part in hidden:
            scaled = (part - mean) * scale * scale_ref[at, 0:1] + scale_ref[at, 1:2]
            parts.append((scaled / (1.0 + jnp.exp(-scaled))).astype(jnp.bfloat16))
        normed.append(jnp.concatenate(parts, axis=1))
    y_ref[0, : TAPS * TILE] = jnp.dot(
        w2_ref[...], jnp.concatenate(normed, axis=0), preferred_element_type=jnp.float32
    )

    def part(tap, lanes):
        return y_ref[0, tap * TILE : (tap + 1) * TILE, lanes]

    low = lax.broadcasted_iota(jnp.int32, (8, LANES), 1) < 64
    layers = out_ref.shape[0] // (2 * tiles)
    for tile, latent in enumerate(tap_sums(part, tiles)):
        turned = pltpu.roll(latent, 64, 1)
        near = jnp.where(low, latent[:8], turned[8:])
        far = jnp.where(low, turned[:8], latent[8:])
        for layer in range(layers):
            out_ref[layer * 2 * tiles + 2 * tile] = near
            out_ref[layer * 2 * tiles + 2 * tile + 1] = far


def share_kernel(
    m0_ref, m1_ref, m2_ref, m3_ref, table_ref, row_ref, merged_ref, base_ref, rope_ref, m_ref
):
    lane = lax.broadcasted_iota(jnp.int32, (16, LANES), 1)
    row = jnp.broadcast_to(row_ref[0], lane.shape).astype(jnp.float32)
    angles = table_ref[:16] * jnp.where((lane < 16) | (lane >= 72), 1.0, row)
    rope_ref[:16] = jnp.cos(angles)
    sine = jnp.sin(angles)
    rope_ref[16:] = jnp.where(lane % 2 == 0, -sine, sine)
    here = lax.axis_index("tm") // 2 * 2 + lax.axis_index("height")
    lines = table_ref[48:56]
    for flip, ref in enumerate((m0_ref, m1_ref, m2_ref, m3_ref)):
        share = ref[...].astype(jnp.float32)
        m_ref[here ^ flip, :, : 4 * LANES] = share[:16]
        m_ref[here ^ flip, :, 4 * LANES :] = share[16:, : 2 * LANES]
        lines = lines + pltpu.roll(share[16:24, 2 * LANES : 3 * LANES], 2, 0)
    base_ref[...] = jnp.concatenate([lines[2 + part : 3 + part] for part in range(6)], axis=1)
    merged_ref[...] = m_ref[...].reshape(merged_ref.shape).astype(jnp.bfloat16)


def token_kernel(p_ref, m_ref, base_ref, rope_ref, table_ref, lat_ref, q_ref, k_ref, v_ref):
    low = lax.broadcasted_iota(jnp.int32, (8, LANES), 1) < 64
    pairs = []
    for side in range(2):
        one, two = (
            sum(p_ref[4 * index + 2 * core + side] for index in range(p_ref.shape[0] // 4))
            for core in range(2)
        )
        top = jnp.where(low, one, pltpu.roll(two, 64, 1))
        bottom = jnp.where(low, pltpu.roll(one, 64, 1), two)
        pairs.append(jnp.concatenate([top, bottom], axis=0))
    total = jnp.concatenate(pairs, axis=1)
    lat = (total + table_ref[32:48, :1]) * latent_scale
    clips = lat.shape[1] // 64
    tokens = clips * 16
    place = lax.axis_index("dp")
    own = lat[:, :LANES]
    for pair in range(1, clips // 2):
        own = jnp.where(place // 2 == pair, lat[:, pair * LANES : (pair + 1) * LANES], own)
    own = jnp.where(place % 2 == 1, pltpu.roll(own, 64, 1), own)
    turned = own.T[:64]
    wide = jnp.concatenate([turned] * 16, axis=1)
    spot = lax.broadcasted_iota(jnp.int32, wide.shape, 0) % 16
    spread = lax.broadcasted_iota(jnp.int32, wide.shape, 1) // 16
    merged = jnp.sum(jnp.where(spot == spread, wide, 0.0).reshape(4, 16, 256), axis=1)
    lat_ref[0, 0] = merged[:2]
    lat_ref[0, 1] = merged[2:]

    lat_bf = lat.astype(jnp.bfloat16)
    token = lax.broadcasted_iota(jnp.int32, (tokens, clips * 64), 0)
    lane = lax.broadcasted_iota(jnp.int32, (tokens, clips * 64), 1)
    first = token // 8 * 32 + token % 8 * 2
    heads = q_ref.shape[2] // HD
    projected = base_ref[...]
    for a in range(2):
        for e in range(2):
            chosen = jnp.where(lane == first + (16 * a + e), 1.0, 0.0).astype(jnp.bfloat16)
            patch = lax.dot_general(
                chosen, lat_bf, (((1,), (1,)), ((), ())), preferred_element_type=jnp.float32
            ).astype(jnp.bfloat16)
            weight = m_ref[(2 * a + e) * TILE : (2 * a + e + 1) * TILE]
            projected = projected + jnp.dot(patch, weight, preferred_element_type=jnp.float32)

    even = lax.broadcasted_iota(jnp.int32, (tokens, HD), 1) % 2 == 0
    cosine = jnp.concatenate([rope_ref[:16]] * clips, axis=0)
    sine = jnp.concatenate([rope_ref[16:]] * clips, axis=0)

    def turn(vectors, gain):
        square = jnp.mean(vectors * vectors, axis=-1, keepdims=True)
        vectors = vectors * lax.rsqrt(square + norm_eps) * gain
        swapped = jnp.where(even, pltpu.roll(vectors, HD - 1, 1), pltpu.roll(vectors, 1, 1))
        return vectors * cosine + swapped * sine

    def keep(ref, head, value):
        value = value.reshape(tokens // 8, 8, HD).astype(jnp.bfloat16)
        ref[:, :, head * HD : (head + 1) * HD] = value

    for head in range(heads):
        at = 3 * HD * head
        keep(q_ref, head, turn(projected[:, at : at + HD], table_ref[48:49]))
        keep(k_ref, head, turn(projected[:, at + HD : at + 2 * HD], table_ref[49:50]))
        keep(v_ref, head, projected[:, at + 2 * HD : at + 3 * HD])


def rope_freqs():
    freqs = []
    for dims in (time_dims, row_dims, row_dims):
        freqs.append(rope_base ** (-np.arange(0, dims, 2, dtype=np.float64) / dims))
    return np.repeat(np.concatenate(freqs), 2)[None].astype(np.float32)


def vmem(count):
    return [pl.BlockSpec(memory_space=pltpu.VMEM)] * count


def grouped(
    clip_inputs,
    conv_in_weight,
    group_gain,
    group_bias,
    conv_out_weight,
    out_bias,
    patch_weight,
    patch_bias,
    qkv_weight,
    qkv_bias,
    q_gain,
    k_gain,
    frame_pos,
    row_pos,
):
    plane_axes = ("tm", "height")
    clips = lax.axis_size("dp")
    steps = lax.axis_size("tm")
    plane = steps * lax.axis_size("height")
    channels = clip_inputs.shape[4]
    depth = conv_in_weight.shape[0]

    width = -(-depth // LANES) * LANES + LANES
    hbm = pl.BlockSpec(memory_space=pltpu.HBM)
    wide = pltpu.CompilerParams(vmem_limit_bytes=60 * 1024 * 1024)
    limit = pltpu.CompilerParams(vmem_limit_bytes=32 * 1024 * 1024)
    small = pl.CostEstimate(flops=10**6, bytes_accessed=10**6, transcendentals=0)
    with jax.named_scope("weight_by_group"):
        weight_block = jax.ShapeDtypeStruct((4 * GROUP, width), jnp.bfloat16)
        own_block = jax.ShapeDtypeStruct((4 * GROUP, width + LANES), jnp.bfloat16)
        small_arrays = (group_gain, group_bias, out_bias, qkv_bias, q_gain, k_gain)
        small_arrays += (frame_pos,)
        *packed, scale, table = pl.pallas_call(
            pack_kernel,
            out_shape=(own_block,)
            + (weight_block,) * 3
            + (
                jax.ShapeDtypeStruct((4 * GROUP, 2), jnp.float32),
                jax.ShapeDtypeStruct((56, LANES), jnp.float32),
            ),
            in_specs=[hbm] * 12,
            out_specs=(hbm,) * 6,
            scratch_shapes=[
                pltpu.VMEM(conv_in_weight.shape, jnp.bfloat16),
                pltpu.VMEM(qkv_weight.shape, jnp.bfloat16),
                pltpu.VMEM((patch_weight.shape[0], qkv_weight.shape[0]), jnp.bfloat16),
                pltpu.VMEM(patch_bias.shape, jnp.bfloat16),
                *[pltpu.VMEM(array.shape, array.dtype) for array in small_arrays],
                pltpu.VMEM((1, HD), jnp.float32),
                pltpu.VMEM((patch_bias.shape[0] // LANES, LANES), jnp.float32),
                pltpu.VMEM((8 * GROUP, depth), jnp.bfloat16),
                pltpu.VMEM((patch_weight.shape[0], qkv_weight.shape[1]), jnp.float32),
                pltpu.VMEM((4, 4 * GROUP, width), jnp.bfloat16),
                pltpu.VMEM((16, LANES), jnp.bfloat16),
                pltpu.VMEM((4 * GROUP, 2), jnp.float32),
                pltpu.VMEM((56, LANES), jnp.float32),
                pltpu.SemaphoreType.DMA((20,)),
            ],
            compiler_params=wide,
            cost_estimate=pl.CostEstimate(flops=10**8, bytes_accessed=10**6, transcendentals=0),
            name="pack_weights",
        )(
            rope_freqs(),
            conv_in_weight,
            qkv_weight,
            patch_weight,
            patch_bias,
            *small_arrays,
        )
        blocks = [packed[0]]
        for flip, block in zip((1, 4, 5), packed[1:]):
            blocks.append(lax.ppermute(block, plane_axes, [(i, i ^ flip) for i in range(plane)]))
    with jax.named_scope("gather_clips"):
        own = clip_inputs.reshape(64, channels)
        layers = []
        for step in reversed(range(clips)):
            pairs = []
            for layer in range(clips):
                for tm in range(steps):
                    to = (layer // 2 * 2 + tm % 2 + step) % clips
                    pair = (layer * steps + tm, to * steps + tm // 2 * 2 + layer % 2)
                    if pair[0] != pair[1]:
                        pairs.append(pair)
            layers.append(lax.ppermute(own, ("dp", "tm"), pairs))
    with jax.named_scope("spread_clips"):
        keep, send = pl.pallas_call(
            arrange_kernel,
            out_shape=(jax.ShapeDtypeStruct((2, 64, channels), jnp.bfloat16),) * 2,
            in_specs=vmem(5),
            out_specs=tuple(vmem(2)),
            scratch_shapes=[pltpu.VMEM((4, 64, channels), jnp.bfloat16)],
            compiler_params=limit,
            cost_estimate=small,
            name="arrange_clips",
        )(*layers, own)
        pieces = [keep]
        for flip in (1, 4, 5):
            pairs = [(i, i ^ flip) for i in range(plane)]
            pieces.append(lax.ppermute(send if flip % 2 else keep, plane_axes, pairs))
    with jax.named_scope("small_weights"):
        first = lax.axis_index("tm") // 2 * (4 * GROUP)
        weight_out = lax.dynamic_slice_in_dim(conv_out_weight, first, 4 * GROUP, axis=1)
        weight_out = weight_out.transpose(0, 2, 1).reshape(TAPS * TILE, 4 * GROUP)
    with jax.named_scope("join_weights"):
        height = len(core_taps(0)) * 4 * GROUP
        joined = pl.pallas_call(
            join_kernel,
            out_shape=jax.ShapeDtypeStruct((height + 32, channels), jnp.bfloat16),
            in_specs=vmem(4),
            out_specs=vmem(1)[0],
            scratch_shapes=[pltpu.VMEM((4, 4 * GROUP, width), jnp.bfloat16)],
            compiler_params=limit,
            cost_estimate=small,
            name="join_weights",
        )(*blocks)
        joined_pair = lax.ppermute(joined, "tm", [(i, i ^ 1) for i in range(steps)])
    with jax.named_scope("merged_projection"):
        share = joined[height:].astype(jnp.float32) + joined_pair[height:].astype(jnp.float32)
        share = share.astype(jnp.bfloat16)
        shares = [share]
        for flip in (1, 4, 5):
            pairs = [(i, i ^ flip) for i in range(plane)]
            shares.append(lax.ppermute(share, plane_axes, pairs))

        merged, base, rope = pl.pallas_call(
            share_kernel,
            out_shape=(
                jax.ShapeDtypeStruct((64, 6 * HD), jnp.bfloat16),
                jax.ShapeDtypeStruct((1, 6 * HD), jnp.float32),
                jax.ShapeDtypeStruct((32, LANES), jnp.float32),
            ),
            in_specs=vmem(5) + [pl.BlockSpec(memory_space=pltpu.SMEM)],
            out_specs=tuple(vmem(3)),
            scratch_shapes=[pltpu.VMEM((4, 16, 6 * HD), jnp.float32)],
            compiler_params=limit,
            cost_estimate=small,
            name="share_rows",
        )(*shares, table, row_pos)

    flops = 4 * height * steps * LANES * channels
    clip = pl.pallas_call(
        place_kernel,
        out_shape=jax.ShapeDtypeStruct((plane, 64, channels), jnp.bfloat16),
        in_specs=vmem(4),
        out_specs=vmem(1)[0],
        compiler_params=limit,
        cost_estimate=pl.CostEstimate(flops=4 * 10**10, bytes_accessed=10**6, transcendentals=0),
        name="place_clip",
    )(*pieces)
    partial = pl.pallas_call(
        conv_kernel,
        out_shape=jax.ShapeDtypeStruct((clips * plane, 8, LANES), jnp.float32),
        in_specs=vmem(5),
        out_specs=vmem(1)[0],
        scratch_shapes=[
            pltpu.VMEM((2, height, steps * LANES), jnp.float32),
        ],
        compiler_params=limit,
        cost_estimate=pl.CostEstimate(flops=flops, bytes_accessed=10**6, transcendentals=0),
        name="convolutions",
    )(clip, joined, joined_pair, scale, weight_out)

    with jax.named_scope("sum_latents"):
        partials = lax.all_to_all(partial, ("dp",) + plane_axes, 0, 0, tiled=True)

    heads = qkv_weight.shape[1] // (3 * HD)
    frames = clip_inputs.shape[1]
    tokens = jax.ShapeDtypeStruct((clips * frames, 8, heads * HD), jnp.bfloat16)
    latents, query, key, value = pl.pallas_call(
        token_kernel,
        out_shape=(jax.ShapeDtypeStruct((1, 2, 2, 256), jnp.float32), tokens, tokens, tokens),
        in_specs=vmem(5),
        out_specs=tuple(vmem(4)),
        compiler_params=limit,
        cost_estimate=pl.CostEstimate(flops=10**8, bytes_accessed=10**6, transcendentals=0),
        name="tokens",
    )(
        partials,
        merged,
        base,
        rope,
        table,
    )
    full = (clips, frames, 1, 8, heads * HD)
    return latents, query.reshape(full), key.reshape(full), value.reshape(full)


def pick(mesh, *arrays):
    if one_group_each(mesh, arrays[0], arrays[1], arrays[4], arrays[8]):
        return grouped(*arrays)
    return shards(*arrays)


def solution(mesh):
    placed = (
        P("dp", "tm", "height", None, None),
        P(("tm", "height"), "dp"),
        P("dp"),
        P("dp"),
        P(None, "dp", None),
        P(),
        P(),
        P(),
        P(("tm", "height"), "dp"),
        P("dp"),
        P(),
        P(),
        P("tm"),
        P("height"),
    )
    return jax.shard_map(
        functools.partial(pick, mesh),
        mesh=mesh,
        in_specs=placed,
        out_specs=(
            P("dp", "tm", "height", None),
            P(None, "tm", "height", None, "dp"),
            P(None, "tm", "height", None, "dp"),
            P(None, "tm", "height", None, "dp"),
        ),
        check_vma=False,
    )
```

profile of v0, /device:TPU:0, one launch (start us, length us, event | category | flops | bytes accessed | tf_op | source)
XLA Modules:
  0.0 45.5 jit_solution(15699714190219108407)
XLA Ops:
  0.6 0.0 copy-start
  0.7 2.7 %pack_weights.1 = (bf16[64,2048]{1,0:T(8,128)(2,1)}, bf16[64,1920]{1,0:T(8,128)(2,1)}, bf16[64,1920]{1,0:T(8,128)(2,1)}, bf16[64,1920]{1,0:T(8,128)(2,1)}, f32[64,2]{1,0:T(8,128)}, /*index=5*/f32[56,128]{1,0:T(8,128)}) custom-call(f32[1,128]{1,0:T(1,128)} %constant.27.clone.freq_hbm, bf16[1728,128]{1,0:T(8,128)(2,1)} %w_hbm.1, bf16[384,768]{1,0:T(8,128)(2,1)} %qkv_hbm.1, ...), custom_call_target="tpu_custom_call" | custom-call | flops 100000000 | bytes 1000000 | tf_op jit(solution)/shard_map/weight_by_group/pack_weights/pallas_call | solution.py:660
  3.4 3.0 %collective-permute-start.7 = (bf16[64,1920]{1,0:T(8,128)(2,1)}, bf16[64,1920]{1,0:T(8,128)(2,1)S(1)}, u32[]{:S(2)}, u32[]{:S(2)}) collective-permute-start(bf16[64,1920]{1,0:T(8,128)(2,1)} %get-tuple-element.22), channel_id=1, source_target_pairs={{0,1},{1,0},{2,3},{3,2},{4,5},{5,4},{6,7},{7,6},{8,9},{9,8},{10,11... | collective-permute-start | bytes 737288 | tf_op jit(solution)/shard_map/weight_by_group/ppermute | solution.py:699
  6.4 3.6 %collective-permute-start = (bf16[64,512]{1,0:T(8,128)(2,1)S(1)}, bf16[64,512]{1,0:T(8,128)(2,1)S(1)}, u32[]{:S(2)}, u32[]{:S(2)}) collective-permute-start(bf16[64,512]{1,0:T(8,128)(2,1)S(1)} %bitcast.14), channel_id=1, source_target_pairs={{0,24},{2,0},{4,28},{6,4},{8,26},{10,2},{12,30},{14,6},{16,8},{18,... | collective-permute-start | bytes 196616 | tf_op jit(solution)/shard_map/gather_clips/ppermute | solution.py:711
  10.0 1.5 %collective-permute-start.8 = (bf16[64,1920]{1,0:T(8,128)(2,1)}, bf16[64,1920]{1,0:T(8,128)(2,1)S(1)}, u32[]{:S(2)}, u32[]{:S(2)}) collective-permute-start(bf16[64,1920]{1,0:T(8,128)(2,1)} %get-tuple-element.23), channel_id=1, source_target_pairs={{0,4},{1,5},{2,6},{3,7},{4,0},{5,1},{6,2},{7,3},{8,12},{9,13},{10,... | collective-permute-start | bytes 737288 | tf_op jit(solution)/shard_map/weight_by_group/ppermute | solution.py:699
  11.5 0.5 %collective-permute-start.9 = (bf16[64,1920]{1,0:T(8,128)(2,1)}, bf16[64,1920]{1,0:T(8,128)(2,1)S(1)}, u32[]{:S(2)}, u32[]{:S(2)}) collective-permute-start(bf16[64,1920]{1,0:T(8,128)(2,1)} %get-tuple-element.24), channel_id=1, source_target_pairs={{0,5},{1,4},{2,7},{3,6},{4,1},{5,0},{6,3},{7,2},{8,13},{9,12},{10,... | collective-permute-start | bytes 737288 | tf_op jit(solution)/shard_map/weight_by_group/ppermute | solution.py:699
  12.0 2.6 %collective-permute-start.2 = (bf16[64,512]{1,0:T(8,128)(2,1)S(1)}, bf16[64,512]{1,0:T(8,128)(2,1)S(1)}, u32[]{:S(2)}, u32[]{:S(2)}) collective-permute-start(bf16[64,512]{1,0:T(8,128)(2,1)S(1)} %bitcast.16), channel_id=1, source_target_pairs={{0,8},{2,16},{4,12},{6,20},{8,10},{10,18},{12,14},{14,22},{16,24},... | collective-permute-start | bytes 196616 | tf_op jit(solution)/shard_map/gather_clips/ppermute | solution.py:711
  14.7 0.6 %collective-permute-done.1.refs_1_ = bf16[64,512]{1,0:T(8,128)(2,1)S(1)} collective-permute-done((bf16[64,512]{1,0:T(8,128)(2,1)S(1)}, bf16[64,512]{1,0:T(8,128)(2,1)S(1)}, u32[]{:S(2)}, u32[]{:S(2)}) %collective-permute-start.1) | collective-permute-done | bytes 65568 | tf_op jit(solution)/shard_map/gather_clips/ppermute | solution.py:711
  15.2 0.7 %collective-permute-start.3 = (bf16[64,512]{1,0:T(8,128)(2,1)S(1)}, bf16[64,512]{1,0:T(8,128)(2,1)S(1)}, u32[]{:S(2)}, u32[]{:S(2)}) collective-permute-start(bf16[64,512]{1,0:T(8,128)(2,1)S(1)} %bitcast.17), channel_id=1, source_target_pairs={{2,8},{6,12},{8,2},{12,6},{18,24},{22,28},{24,18},{28,22},{3,9},{7... | collective-permute-start | bytes 196616 | tf_op jit(solution)/shard_map/gather_clips/ppermute | solution.py:711
  15.9 1.4 %collective-permute-done.2.refs_2_ = bf16[64,512]{1,0:T(8,128)(2,1)S(1)} collective-permute-done((bf16[64,512]{1,0:T(8,128)(2,1)S(1)}, bf16[64,512]{1,0:T(8,128)(2,1)S(1)}, u32[]{:S(2)}, u32[]{:S(2)}) %collective-permute-start.2) | collective-permute-done | bytes 65568 | tf_op jit(solution)/shard_map/gather_clips/ppermute | solution.py:711
  17.3 0.1 arrange_clips.1
  17.4 1.6 %collective-permute-start.4 = (bf16[2,64,512]{2,1,0:T(8,128)(2,1)S(1)}, bf16[2,64,512]{2,1,0:T(8,128)(2,1)S(1)}, u32[]{:S(2)}, u32[]{:S(2)}) collective-permute-start(bf16[2,64,512]{2,1,0:T(8,128)(2,1)S(1)} %get-tuple-element.20), channel_id=1, source_target_pairs={{0,1},{1,0},{2,3},{3,2},{4,5},{5,4},{6,7},{7,6},{8,9},{9,8},{10,11... | collective-permute-start | bytes 393224 | tf_op jit(solution)/shard_map/spread_clips/ppermute | solution.py:726
  19.0 1.5 %collective-permute-start.5 = (bf16[2,64,512]{2,1,0:T(8,128)(2,1)S(1)}, bf16[2,64,512]{2,1,0:T(8,128)(2,1)S(1)}, u32[]{:S(2)}, u32[]{:S(2)}) collective-permute-start(bf16[2,64,512]{2,1,0:T(8,128)(2,1)S(1)} %get-tuple-element.19.refs_0_), channel_id=1, source_target_pairs={{0,4},{1,5},{2,6},{3,7},{4,0},{5,1},{6,2},{7,3},{8,12},{9,13},{10,... | collective-permute-start | bytes 393224 | tf_op jit(solution)/shard_map/spread_clips/ppermute | solution.py:726
  20.5 0.5 %collective-permute-start.6 = (bf16[2,64,512]{2,1,0:T(8,128)(2,1)S(1)}, bf16[2,64,512]{2,1,0:T(8,128)(2,1)S(1)}, u32[]{:S(2)}, u32[]{:S(2)}) collective-permute-start(bf16[2,64,512]{2,1,0:T(8,128)(2,1)S(1)} %get-tuple-element.20), channel_id=1, source_target_pairs={{0,5},{1,4},{2,7},{3,6},{4,1},{5,0},{6,3},{7,2},{8,13},{9,12},{10,... | collective-permute-start | bytes 393224 | tf_op jit(solution)/shard_map/spread_clips/ppermute | solution.py:726
  21.0 0.1 constant_dynamic-slice_fusion
  21.1 2.5 %collective-permute-done.8.high_ref = bf16[64,1920]{1,0:T(8,128)(2,1)S(1)} collective-permute-done((bf16[64,1920]{1,0:T(8,128)(2,1)}, bf16[64,1920]{1,0:T(8,128)(2,1)S(1)}, u32[]{:S(2)}, u32[]{:S(2)}) %collective-permute-start.8) | collective-permute-done | bytes 245792 | tf_op jit(solution)/shard_map/weight_by_group/ppermute | solution.py:699
  23.5 0.4 join_weights.1.wt_ref
  23.9 0.4 collective-permute-start.10
  24.3 1.0 %collective-permute-done.5.refs_2_ = bf16[2,64,512]{2,1,0:T(8,128)(2,1)S(1)} collective-permute-done((bf16[2,64,512]{2,1,0:T(8,128)(2,1)S(1)}, bf16[2,64,512]{2,1,0:T(8,128)(2,1)S(1)}, u32[]{:S(2)}, u32[]{:S(2)}) %collective-permute-start.5) | collective-permute-done | bytes 131104 | tf_op jit(solution)/shard_map/spread_clips/ppermute | solution.py:726
  25.3 2.5 %collective-permute-done.6.refs_3_ = bf16[2,64,512]{2,1,0:T(8,128)(2,1)S(1)} collective-permute-done((bf16[2,64,512]{2,1,0:T(8,128)(2,1)S(1)}, bf16[2,64,512]{2,1,0:T(8,128)(2,1)S(1)}, u32[]{:S(2)}, u32[]{:S(2)}) %collective-permute-start.6) | collective-permute-done | bytes 131104 | tf_op jit(solution)/shard_map/spread_clips/ppermute | solution.py:726
  27.8 0.1 place_clip.1.x_ref
  27.9 3.6 %convolutions.1 = f32[32,8,128]{2,1,0:T(8,128)} custom-call(bf16[8,64,512]{2,1,0:T(8,128)(2,1)S(1)} %place_clip.1.x_ref, bf16[992,512]{1,0:T(8,128)(2,1)S(1)} %join_weights.1.wt_ref, bf16[992,512]{1,0:T(8,128)(2,1)S(1)} %collective-permute-done.10.pair_ref, f32[64,2]{1,0:T(8,128)S(1)} %copy-done.4, bf16[432,64]{1,0:T(8,128)(2,1)S(1)} %bitcast.13), custom_call_target="tpu_custom_call" | custom-call | flops 1006632960 | bytes 1000000 | tf_op jit(solution)/shard_map/convolutions/pallas_call | solution.py:777
  31.6 3.7 %all-to-all-start = ((f32[32,8,128]{2,1,0:T(8,128)}), f32[32,8,128]{2,1,0:T(8,128)S(1)}, u32[]{:S(2)}, u32[]{:S(2)}) async-start(f32[32,8,128]{2,1,0:T(8,128)} %convolutions.1), calls=%async_computation | async-start | bytes 262144 | tf_op jit(solution)/shard_map/sum_latents/all_to_all | solution.py:791
  35.2 0.0 copy-start.3
  35.3 1.8 %collective-permute-start.11 = (bf16[32,512]{1,0:T(8,128)(2,1)S(1)}, bf16[32,512]{1,0:T(8,128)(2,1)S(1)}, u32[]{:S(2)}, u32[]{:S(2)}) collective-permute-start(bf16[32,512]{1,0:T(8,128)(2,1)S(1)} %add_convert_fusion.m0_ref), channel_id=1, source_target_pairs={{0,1},{1,0},{2,3},{3,2},{4,5},{5,4},{6,7},{7,6},{8,9},{9,8},{10,11... | collective-permute-start | bytes 98312 | tf_op jit(solution)/shard_map/merged_projection/ppermute | solution.py:750
  37.1 1.5 %collective-permute-start.12 = (bf16[32,512]{1,0:T(8,128)(2,1)S(1)}, bf16[32,512]{1,0:T(8,128)(2,1)S(1)}, u32[]{:S(2)}, u32[]{:S(2)}) collective-permute-start(bf16[32,512]{1,0:T(8,128)(2,1)S(1)} %add_convert_fusion.m0_ref), channel_id=1, source_target_pairs={{0,4},{1,5},{2,6},{3,7},{4,0},{5,1},{6,2},{7,3},{8,12},{9,13},{10,... | collective-permute-start | bytes 98312 | tf_op jit(solution)/shard_map/merged_projection/ppermute | solution.py:750
  38.6 0.3 collective-permute-start.13
  39.5 1.7 %collective-permute-done.12.m2_ref = bf16[32,512]{1,0:T(8,128)(2,1)S(1)} collective-permute-done((bf16[32,512]{1,0:T(8,128)(2,1)S(1)}, bf16[32,512]{1,0:T(8,128)(2,1)S(1)}, u32[]{:S(2)}, u32[]{:S(2)}) %collective-permute-start.12) | collective-permute-done | bytes 32800 | tf_op jit(solution)/shard_map/merged_projection/ppermute | solution.py:750
  41.2 2.3 %collective-permute-done.13.m3_ref = bf16[32,512]{1,0:T(8,128)(2,1)S(1)} collective-permute-done((bf16[32,512]{1,0:T(8,128)(2,1)S(1)}, bf16[32,512]{1,0:T(8,128)(2,1)S(1)}, u32[]{:S(2)}, u32[]{:S(2)}) %collective-permute-start.13) | collective-permute-done | bytes 32800 | tf_op jit(solution)/shard_map/merged_projection/ppermute | solution.py:750
  43.5 0.1 share_rows.1
  43.5 0.3 all-to-all-done.p_ref
  43.9 1.6 %tokens.1 = (f32[1,2,2,256]{3,2,1,0:T(2,128)}, bf16[8,8,256]{2,1,0:T(8,128)(2,1)}, bf16[8,8,256]{2,1,0:T(8,128)(2,1)}, bf16[8,8,256]{2,1,0:T(8,128)(2,1)}) custom-call(f32[32,8,128]{2,1,0:T(8,128)S(1)} %all-to-all-done.p_ref, bf16[64,768]{1,0:T(8,128)(2,1)S(1)} %get-tuple-element.27.m_ref, f32[1,768]{1,0:T(1,128)S(1)} %get-tuple-element.28.base_ref, ...), custom_call_target="tpu_custom_call" | custom-call | flops 100000000 | bytes 1000000 | tf_op jit(solution)/shard_map/tokens/pallas_call | solution.py:796
  (17 shorter events, 0.0 us)
Async XLA Ops:
  0.6 20.3 %copy-start = (bf16[27,128,16]{1,2,0:T(8,128)(2,1)S(1)}, bf16[27,128,16]{1,2,0:T(8,128)(2,1)}, u32[]{:S(2)}) copy-start(bf16[27,128,16]{1,2,0:T(8,128)(2,1)} %param.19) | copy-start | bytes 331780
  0.7 5.8 %copy-start.2 = (bf16[1,2,2,16,512]{4,3,2,1,0:T(8,128)(2,1)S(1)}, bf16[1,2,2,16,512]{4,3,2,1,0:T(8,128)(2,1)}, u32[]{:S(2)}) copy-start(bf16[1,2,2,16,512]{4,3,2,1,0:T(8,128)(2,1)} %param.15) | copy-start | bytes 196612
  3.4 17.1 %collective-permute-start.7 = (bf16[64,1920]{1,0:T(8,128)(2,1)}, bf16[64,1920]{1,0:T(8,128)(2,1)S(1)}, u32[]{:S(2)}, u32[]{:S(2)}) collective-permute-start(bf16[64,1920]{1,0:T(8,128)(2,1)} %get-tuple-element.22), channel_id=1, source_target_pairs={{0,1},{1,0},{2,3},{3,2},{4,5},{5,4},{6,7},{7,6},{8,9},{9,8},{10,11... | collective-permute-start | bytes 737288 | tf_op jit(solution)/shard_map/weight_by_group/ppermute | solution.py:699
  6.4 5.6 %collective-permute-start = (bf16[64,512]{1,0:T(8,128)(2,1)S(1)}, bf16[64,512]{1,0:T(8,128)(2,1)S(1)}, u32[]{:S(2)}, u32[]{:S(2)}) collective-permute-start(bf16[64,512]{1,0:T(8,128)(2,1)S(1)} %bitcast.14), channel_id=1, source_target_pairs={{0,24},{2,0},{4,28},{6,4},{8,26},{10,2},{12,30},{14,6},{16,8},{18,... | collective-permute-start | bytes 196616 | tf_op jit(solution)/shard_map/gather_clips/ppermute | solution.py:711
  10.0 5.2 %collective-permute-start.1 = (bf16[64,512]{1,0:T(8,128)(2,1)S(1)}, bf16[64,512]{1,0:T(8,128)(2,1)S(1)}, u32[]{:S(2)}, u32[]{:S(2)}) collective-permute-start(bf16[64,512]{1,0:T(8,128)(2,1)S(1)} %bitcast.15), channel_id=1, source_target_pairs={{0,16},{2,24},{4,20},{6,28},{8,18},{10,26},{12,22},{14,30},{16,0},... | collective-permute-start | bytes 196616 | tf_op jit(solution)/shard_map/gather_clips/ppermute | solution.py:711
  10.0 13.5 %collective-permute-start.8 = (bf16[64,1920]{1,0:T(8,128)(2,1)}, bf16[64,1920]{1,0:T(8,128)(2,1)S(1)}, u32[]{:S(2)}, u32[]{:S(2)}) collective-permute-start(bf16[64,1920]{1,0:T(8,128)(2,1)} %get-tuple-element.23), channel_id=1, source_target_pairs={{0,4},{1,5},{2,6},{3,7},{4,0},{5,1},{6,2},{7,3},{8,12},{9,13},{10,... | collective-permute-start | bytes 737288 | tf_op jit(solution)/shard_map/weight_by_group/ppermute | solution.py:699
  11.5 12.0 %copy-start.1 = (bf16[64,2048]{1,0:T(8,128)(2,1)S(1)}, bf16[64,2048]{1,0:T(8,128)(2,1)}, u32[]{:S(2)}) copy-start(bf16[64,2048]{1,0:T(8,128)(2,1)} %get-tuple-element.21.own_ref) | copy-start | bytes 786436
  11.5 12.0 %collective-permute-start.9 = (bf16[64,1920]{1,0:T(8,128)(2,1)}, bf16[64,1920]{1,0:T(8,128)(2,1)S(1)}, u32[]{:S(2)}, u32[]{:S(2)}) collective-permute-start(bf16[64,1920]{1,0:T(8,128)(2,1)} %get-tuple-element.24), channel_id=1, source_target_pairs={{0,5},{1,4},{2,7},{3,6},{4,1},{5,0},{6,3},{7,2},{8,13},{9,12},{10,... | collective-permute-start | bytes 737288 | tf_op jit(solution)/shard_map/weight_by_group/ppermute | solution.py:699
  12.0 5.3 %collective-permute-start.2 = (bf16[64,512]{1,0:T(8,128)(2,1)S(1)}, bf16[64,512]{1,0:T(8,128)(2,1)S(1)}, u32[]{:S(2)}, u32[]{:S(2)}) collective-permute-start(bf16[64,512]{1,0:T(8,128)(2,1)S(1)} %bitcast.16), channel_id=1, source_target_pairs={{0,8},{2,16},{4,12},{6,20},{8,10},{10,18},{12,14},{14,22},{16,24},... | collective-permute-start | bytes 196616 | tf_op jit(solution)/shard_map/gather_clips/ppermute | solution.py:711
  15.2 2.1 %collective-permute-start.3 = (bf16[64,512]{1,0:T(8,128)(2,1)S(1)}, bf16[64,512]{1,0:T(8,128)(2,1)S(1)}, u32[]{:S(2)}, u32[]{:S(2)}) collective-permute-start(bf16[64,512]{1,0:T(8,128)(2,1)S(1)} %bitcast.17), channel_id=1, source_target_pairs={{2,8},{6,12},{8,2},{12,6},{18,24},{22,28},{24,18},{28,22},{3,9},{7... | collective-permute-start | bytes 196616 | tf_op jit(solution)/shard_map/gather_clips/ppermute | solution.py:711
  17.4 6.9 %collective-permute-start.4 = (bf16[2,64,512]{2,1,0:T(8,128)(2,1)S(1)}, bf16[2,64,512]{2,1,0:T(8,128)(2,1)S(1)}, u32[]{:S(2)}, u32[]{:S(2)}) collective-permute-start(bf16[2,64,512]{2,1,0:T(8,128)(2,1)S(1)} %get-tuple-element.20), channel_id=1, source_target_pairs={{0,1},{1,0},{2,3},{3,2},{4,5},{5,4},{6,7},{7,6},{8,9},{9,8},{10,11... | collective-permute-start | bytes 393224 | tf_op jit(solution)/shard_map/spread_clips/ppermute | solution.py:726
  19.0 6.4 %collective-permute-start.5 = (bf16[2,64,512]{2,1,0:T(8,128)(2,1)S(1)}, bf16[2,64,512]{2,1,0:T(8,128)(2,1)S(1)}, u32[]{:S(2)}, u32[]{:S(2)}) collective-permute-start(bf16[2,64,512]{2,1,0:T(8,128)(2,1)S(1)} %get-tuple-element.19.refs_0_), channel_id=1, source_target_pairs={{0,4},{1,5},{2,6},{3,7},{4,0},{5,1},{6,2},{7,3},{8,12},{9,13},{10,... | collective-permute-start | bytes 393224 | tf_op jit(solution)/shard_map/spread_clips/ppermute | solution.py:726
  20.5 7.4 %collective-permute-start.6 = (bf16[2,64,512]{2,1,0:T(8,128)(2,1)S(1)}, bf16[2,64,512]{2,1,0:T(8,128)(2,1)S(1)}, u32[]{:S(2)}, u32[]{:S(2)}) collective-permute-start(bf16[2,64,512]{2,1,0:T(8,128)(2,1)S(1)} %get-tuple-element.20), channel_id=1, source_target_pairs={{0,5},{1,4},{2,7},{3,6},{4,1},{5,0},{6,3},{7,2},{8,13},{9,12},{10,... | collective-permute-start | bytes 393224 | tf_op jit(solution)/shard_map/spread_clips/ppermute | solution.py:726
  23.9 4.0 %copy-start.4 = (f32[64,2]{1,0:T(8,128)S(1)}, f32[64,2]{1,0:T(8,128)}, u32[]{:S(2)}) copy-start(f32[64,2]{1,0:T(8,128)} %get-tuple-element.25.scale_ref) | copy-start | bytes 1540
  23.9 4.0 %collective-permute-start.10 = (bf16[992,512]{1,0:T(8,128)(2,1)S(1)}, bf16[992,512]{1,0:T(8,128)(2,1)S(1)}, u32[]{:S(2)}, u32[]{:S(2)}) collective-permute-start(bf16[992,512]{1,0:T(8,128)(2,1)S(1)} %join_weights.1.wt_ref), channel_id=1, source_target_pairs={{0,2},{2,0},{4,6},{6,4},{1,3},{3,1},{5,7},{7,5},{8,10},{10,8},{12,... | collective-permute-start | bytes 3047432 | tf_op jit(solution)/shard_map/join_weights/ppermute | solution.py:743
  31.6 12.3 %all-to-all-start = ((f32[32,8,128]{2,1,0:T(8,128)}), f32[32,8,128]{2,1,0:T(8,128)S(1)}, u32[]{:S(2)}, u32[]{:S(2)}) async-start(f32[32,8,128]{2,1,0:T(8,128)} %convolutions.1), calls=%async_computation | async-start | bytes 262144 | tf_op jit(solution)/shard_map/sum_latents/all_to_all | solution.py:791
  35.2 8.2 %copy-start.3 = (f32[56,128]{1,0:T(8,128)S(1)}, f32[56,128]{1,0:T(8,128)}, u32[]{:S(2)}) copy-start(f32[56,128]{1,0:T(8,128)} %get-tuple-element.26.table_ref) | copy-start | bytes 86020
  35.3 4.2 %collective-permute-start.11 = (bf16[32,512]{1,0:T(8,128)(2,1)S(1)}, bf16[32,512]{1,0:T(8,128)(2,1)S(1)}, u32[]{:S(2)}, u32[]{:S(2)}) collective-permute-start(bf16[32,512]{1,0:T(8,128)(2,1)S(1)} %add_convert_fusion.m0_ref), channel_id=1, source_target_pairs={{0,1},{1,0},{2,3},{3,2},{4,5},{5,4},{6,7},{7,6},{8,9},{9,8},{10,11... | collective-permute-start | bytes 98312 | tf_op jit(solution)/shard_map/merged_projection/ppermute | solution.py:750
  37.1 4.1 %collective-permute-start.12 = (bf16[32,512]{1,0:T(8,128)(2,1)S(1)}, bf16[32,512]{1,0:T(8,128)(2,1)S(1)}, u32[]{:S(2)}, u32[]{:S(2)}) collective-permute-start(bf16[32,512]{1,0:T(8,128)(2,1)S(1)} %add_convert_fusion.m0_ref), channel_id=1, source_target_pairs={{0,4},{1,5},{2,6},{3,7},{4,0},{5,1},{6,2},{7,3},{8,12},{9,13},{10,... | collective-permute-start | bytes 98312 | tf_op jit(solution)/shard_map/merged_projection/ppermute | solution.py:750
  38.6 4.9 %collective-permute-start.13 = (bf16[32,512]{1,0:T(8,128)(2,1)S(1)}, bf16[32,512]{1,0:T(8,128)(2,1)S(1)}, u32[]{:S(2)}, u32[]{:S(2)}) collective-permute-start(bf16[32,512]{1,0:T(8,128)(2,1)S(1)} %add_convert_fusion.m0_ref), channel_id=1, source_target_pairs={{0,5},{1,4},{2,7},{3,6},{4,1},{5,0},{6,3},{7,2},{8,13},{9,12},{10,... | collective-permute-start | bytes 98312 | tf_op jit(solution)/shard_map/merged_projection/ppermute | solution.py:750
where the time goes:
time: 45.7 us; the launch traced here: 45.5 us
  starting transfers between devices  23 us (50%)
  waiting for transfers between devices  12.3 us (27%)
  Pallas kernels  8.6 us (19%)
  between operations  1.41 us (3%)
    ppermute x4, starting transfers between devices, grouped(): layers.append(lax.ppermute(own, ('dp', 'tm'), pairs))  6.88 us
    ppermute x3, starting transfers between devices, grouped(): lax.ppermute(block, plane_axes, [(i, i ^ flip) for i in range(plane)])  5 us
    ppermute x3, waiting for transfers between devices, grouped(): shares.append(lax.ppermute(share, plane_axes, pairs))  3.99 us
    all_to_all x1, starting transfers between devices, grouped(): partials = lax.all_to_all(partial, ('dp',) + plane_axes, 0, 0, tiled=True)  3.67 us
    pallas_call x1, Pallas kernels, grouped(): pl.pallas_call(conv_kernel, out_shape=jax.ShapeDtypeStruct((clips * plane...  3.64 us
    ppermute x3, starting transfers between devices, grouped(): pieces.append(lax.ppermute(send if flip % 2 else keep, plane_axes, pairs))  3.55 us
    ppermute x3, starting transfers between devices, grouped(): shares.append(lax.ppermute(share, plane_axes, pairs))  3.55 us
    ppermute x3, waiting for transfers between devices, grouped(): pieces.append(lax.ppermute(send if flip % 2 else keep, plane_axes, pairs))  3.54 us
  transfers between devices with their start and end apart: 15, of which 8 were waited for; matrix products, arithmetic and copies ran while one was open for 0% of the time, Pallas kernels for 1%

commit v1 on v0

--- a/solution.py
+++ b/solution.py
@@ -706,8 +706,9 @@
                 for tm in range(steps):
                     to = (layer // 2 * 2 + tm % 2 + step) % clips
                     pair = (layer * steps + tm, to * steps + tm // 2 * 2 + layer % 2)
-                    if pair[0] != pair[1]:
-                        pairs.append(pair)
+                    if pair[0] == pair[1]:
+                        pair = (pair[0], (layer ^ 1) * steps + (tm ^ 1))
+                    pairs.append(pair)
             layers.append(lax.ppermute(own, ("dp", "tm"), pairs))
     with jax.named_scope("spread_clips"):
         keep, send = pl.pallas_call(

time: 45.7 us -> 46.6 us (1.020)
  waiting for transfers between devices: 12.3 us -> 14.6 us
  starting transfers between devices: 23 us -> 21.7 us
    ppermute x4, waiting for transfers between devices: 2.01 us -> 4.91 us  [grouped(): layers.append(lax.ppermute(own, ('dp', 'tm'), pairs))]
    ppermute x3, waiting for transfers between devices: 2.46 us -> 0.67 us  [grouped(): lax.ppermute(block, plane_axes, [(i, i ^ flip) for i in range(plane)])]
    ppermute x3, waiting for transfers between devices: 3.54 us -> 4.7 us  [grouped(): pieces.append(lax.ppermute(send if flip % 2 else keep, plane_axes, pairs))]
    ppermute x4, starting transfers between devices: 6.88 us -> 6.23 us  [grouped(): layers.append(lax.ppermute(own, ('dp', 'tm'), pairs))]
  transfers between devices with their start and end apart: 15 -> 15, of which waited for: 8 -> 9; matrix products, arithmetic and copies ran while one was open for 0% -> 0% of each run, Pallas kernels for 1% -> 1%
where the time goes in v1:
time: 46.6 us; the launch traced here: 46.4 us
  starting transfers between devices  21.7 us (47%)
  waiting for transfers between devices  14.6 us (31%)
  Pallas kernels  8.6 us (18%)
  between operations  1.41 us (3%)
    ppermute x4, starting transfers between devices, grouped(): layers.append(lax.ppermute(own, ('dp', 'tm'), pairs))  6.23 us
    ppermute x3, starting transfers between devices, grouped(): lax.ppermute(block, plane_axes, [(i, i ^ flip) for i in range(plane)])  5 us
    ppermute x4, waiting for transfers between devices, grouped(): layers.append(lax.ppermute(own, ('dp', 'tm'), pairs))  4.91 us
    ppermute x3, waiting for transfers between devices, grouped(): pieces.append(lax.ppermute(send if flip % 2 else keep, plane_axes, pairs))  4.7 us
    ppermute x3, waiting for transfers between devices, grouped(): shares.append(lax.ppermute(share, plane_axes, pairs))  3.99 us
    pallas_call x1, Pallas kernels, grouped(): pl.pallas_call(conv_kernel, out_shape=jax.ShapeDtypeStruct((clips * plane...  3.64 us
    ppermute x3, starting transfers between devices, grouped(): shares.append(lax.ppermute(share, plane_axes, pairs))  3.55 us
    ppermute x3, starting transfers between devices, grouped(): pieces.append(lax.ppermute(send if flip % 2 else keep, plane_axes, pairs))  3.55 us
  transfers between devices with their start and end apart: 15, of which 9 were waited for; matrix products, arithmetic and copies ran while one was open for 0% of the time, Pallas kernels for 1%

profile of v1, /device:TPU:0, one launch (start us, length us, event | category | flops | bytes accessed | tf_op | source)
XLA Modules:
  0.0 46.4 jit_solution(14012542544478884210)
XLA Ops:
  0.6 0.0 copy-start
  0.7 2.7 %pack_weights.1 = (bf16[64,2048]{1,0:T(8,128)(2,1)}, bf16[64,1920]{1,0:T(8,128)(2,1)}, bf16[64,1920]{1,0:T(8,128)(2,1)}, bf16[64,1920]{1,0:T(8,128)(2,1)}, f32[64,2]{1,0:T(8,128)}, /*index=5*/f32[56,128]{1,0:T(8,128)}) custom-call(f32[1,128]{1,0:T(1,128)} %constant.27.clone.freq_hbm, bf16[1728,128]{1,0:T(8,128)(2,1)} %w_hbm.1, bf16[384,768]{1,0:T(8,128)(2,1)} %qkv_hbm.1, ...), custom_call_target="tpu_custom_call" | custom-call | flops 100000000 | bytes 1000000 | tf_op jit(solution)/shard_map/weight_by_group/pack_weights/pallas_call | solution.py:660
  3.4 3.0 %collective-permute-start.7 = (bf16[64,1920]{1,0:T(8,128)(2,1)}, bf16[64,1920]{1,0:T(8,128)(2,1)S(1)}, u32[]{:S(2)}, u32[]{:S(2)}) collective-permute-start(bf16[64,1920]{1,0:T(8,128)(2,1)} %get-tuple-element.22), channel_id=1, source_target_pairs={{0,1},{1,0},{2,3},{3,2},{4,5},{5,4},{6,7},{7,6},{8,9},{9,8},{10,11... | collective-permute-start | bytes 737288 | tf_op jit(solution)/shard_map/weight_by_group/ppermute | solution.py:699
  6.4 3.6 %collective-permute-start = (bf16[64,512]{1,0:T(8,128)(2,1)S(1)}, bf16[64,512]{1,0:T(8,128)(2,1)S(1)}, u32[]{:S(2)}, u32[]{:S(2)}) collective-permute-start(bf16[64,512]{1,0:T(8,128)(2,1)S(1)} %bitcast.14), channel_id=1, source_target_pairs={{0,24},{2,0},{4,28},{6,4},{8,26},{10,2},{12,30},{14,6},{16,8},{18,... | collective-permute-start | bytes 196616 | tf_op jit(solution)/shard_map/gather_clips/ppermute | solution.py:712
  10.0 1.5 %collective-permute-start.8 = (bf16[64,1920]{1,0:T(8,128)(2,1)}, bf16[64,1920]{1,0:T(8,128)(2,1)S(1)}, u32[]{:S(2)}, u32[]{:S(2)}) collective-permute-start(bf16[64,1920]{1,0:T(8,128)(2,1)} %get-tuple-element.23), channel_id=1, source_target_pairs={{0,4},{1,5},{2,6},{3,7},{4,0},{5,1},{6,2},{7,3},{8,12},{9,13},{10,... | collective-permute-start | bytes 737288 | tf_op jit(solution)/shard_map/weight_by_group/ppermute | solution.py:699
  11.5 0.5 %collective-permute-start.9 = (bf16[64,1920]{1,0:T(8,128)(2,1)}, bf16[64,1920]{1,0:T(8,128)(2,1)S(1)}, u32[]{:S(2)}, u32[]{:S(2)}) collective-permute-start(bf16[64,1920]{1,0:T(8,128)(2,1)} %get-tuple-element.24), channel_id=1, source_target_pairs={{0,5},{1,4},{2,7},{3,6},{4,1},{5,0},{6,3},{7,2},{8,13},{9,12},{10,... | collective-permute-start | bytes 737288 | tf_op jit(solution)/shard_map/weight_by_group/ppermute | solution.py:699
  12.0 2.6 %collective-permute-start.2 = (bf16[64,512]{1,0:T(8,128)(2,1)S(1)}, bf16[64,512]{1,0:T(8,128)(2,1)S(1)}, u32[]{:S(2)}, u32[]{:S(2)}) collective-permute-start(bf16[64,512]{1,0:T(8,128)(2,1)S(1)} %bitcast.16), channel_id=1, source_target_pairs={{0,8},{2,16},{4,12},{6,20},{8,10},{10,18},{12,14},{14,22},{16,24},... | collective-permute-start | bytes 196616 | tf_op jit(solution)/shard_map/gather_clips/ppermute | solution.py:712
  14.7 0.6 %collective-permute-done.1.refs_1_ = bf16[64,512]{1,0:T(8,128)(2,1)S(1)} collective-permute-done((bf16[64,512]{1,0:T(8,128)(2,1)S(1)}, bf16[64,512]{1,0:T(8,128)(2,1)S(1)}, u32[]{:S(2)}, u32[]{:S(2)}) %collective-permute-start.1) | collective-permute-done | bytes 65568 | tf_op jit(solution)/shard_map/gather_clips/ppermute | solution.py:712
  15.2 2.1 %collective-permute-done.2.refs_2_ = bf16[64,512]{1,0:T(8,128)(2,1)S(1)} collective-permute-done((bf16[64,512]{1,0:T(8,128)(2,1)S(1)}, bf16[64,512]{1,0:T(8,128)(2,1)S(1)}, u32[]{:S(2)}, u32[]{:S(2)}) %collective-permute-start.2) | collective-permute-done | bytes 65568 | tf_op jit(solution)/shard_map/gather_clips/ppermute | solution.py:712
  17.3 2.2 %collective-permute-done.3.refs_3_ = bf16[64,512]{1,0:T(8,128)(2,1)S(1)} collective-permute-done((bf16[64,512]{1,0:T(8,128)(2,1)S(1)}, bf16[64,512]{1,0:T(8,128)(2,1)S(1)}, u32[]{:S(2)}, u32[]{:S(2)}) %collective-permute-start.3) | collective-permute-done | bytes 65568 | tf_op jit(solution)/shard_map/gather_clips/ppermute | solution.py:712
  19.6 0.1 arrange_clips.1
  19.6 0.1 collective-permute-start.4
  19.7 1.6 %collective-permute-start.5 = (bf16[2,64,512]{2,1,0:T(8,128)(2,1)S(1)}, bf16[2,64,512]{2,1,0:T(8,128)(2,1)S(1)}, u32[]{:S(2)}, u32[]{:S(2)}) collective-permute-start(bf16[2,64,512]{2,1,0:T(8,128)(2,1)S(1)} %get-tuple-element.19.refs_0_), channel_id=1, source_target_pairs={{0,4},{1,5},{2,6},{3,7},{4,0},{5,1},{6,2},{7,3},{8,12},{9,13},{10,... | collective-permute-start | bytes 393224 | tf_op jit(solution)/shard_map/spread_clips/ppermute | solution.py:727
  21.3 1.9 %collective-permute-start.6 = (bf16[2,64,512]{2,1,0:T(8,128)(2,1)S(1)}, bf16[2,64,512]{2,1,0:T(8,128)(2,1)S(1)}, u32[]{:S(2)}, u32[]{:S(2)}) collective-permute-start(bf16[2,64,512]{2,1,0:T(8,128)(2,1)S(1)} %get-tuple-element.20), channel_id=1, source_target_pairs={{0,5},{1,4},{2,7},{3,6},{4,1},{5,0},{6,3},{7,2},{8,13},{9,12},{10,... | collective-permute-start | bytes 393224 | tf_op jit(solution)/shard_map/spread_clips/ppermute | solution.py:727
  23.2 0.1 constant_dynamic-slice_fusion
  23.3 0.7 %collective-permute-done.8.high_ref = bf16[64,1920]{1,0:T(8,128)(2,1)S(1)} collective-permute-done((bf16[64,1920]{1,0:T(8,128)(2,1)}, bf16[64,1920]{1,0:T(8,128)(2,1)S(1)}, u32[]{:S(2)}, u32[]{:S(2)}) %collective-permute-start.8) | collective-permute-done | bytes 245792 | tf_op jit(solution)/shard_map/weight_by_group/ppermute | solution.py:699
  24.0 0.4 join_weights.1.wt_ref
  24.4 0.0 collective-permute-start.10
  24.4 1.6 %collective-permute-done.4.refs_1_ = bf16[2,64,512]{2,1,0:T(8,128)(2,1)S(1)} collective-permute-done((bf16[2,64,512]{2,1,0:T(8,128)(2,1)S(1)}, bf16[2,64,512]{2,1,0:T(8,128)(2,1)S(1)}, u32[]{:S(2)}, u32[]{:S(2)}) %collective-permute-start.4) | collective-permute-done | bytes 131104 | tf_op jit(solution)/shard_map/spread_clips/ppermute | solution.py:727
  26.0 3.1 %collective-permute-done.5.refs_2_ = bf16[2,64,512]{2,1,0:T(8,128)(2,1)S(1)} collective-permute-done((bf16[2,64,512]{2,1,0:T(8,128)(2,1)S(1)}, bf16[2,64,512]{2,1,0:T(8,128)(2,1)S(1)}, u32[]{:S(2)}, u32[]{:S(2)}) %collective-permute-start.5) | collective-permute-done | bytes 131104 | tf_op jit(solution)/shard_map/spread_clips/ppermute | solution.py:727
  29.1 0.1 place_clip.1.x_ref
  29.2 3.6 %convolutions.1 = f32[32,8,128]{2,1,0:T(8,128)} custom-call(bf16[8,64,512]{2,1,0:T(8,128)(2,1)S(1)} %place_clip.1.x_ref, bf16[992,512]{1,0:T(8,128)(2,1)S(1)} %join_weights.1.wt_ref, bf16[992,512]{1,0:T(8,128)(2,1)S(1)} %collective-permute-done.10.pair_ref, f32[64,2]{1,0:T(8,128)S(1)} %copy-done.4, bf16[432,64]{1,0:T(8,128)(2,1)S(1)} %bitcast.13), custom_call_target="tpu_custom_call" | custom-call | flops 1006632960 | bytes 1000000 | tf_op jit(solution)/shard_map/convolutions/pallas_call | solution.py:778
  32.9 3.3 %all-to-all-start = ((f32[32,8,128]{2,1,0:T(8,128)}), f32[32,8,128]{2,1,0:T(8,128)S(1)}, u32[]{:S(2)}, u32[]{:S(2)}) async-start(f32[32,8,128]{2,1,0:T(8,128)} %convolutions.1), calls=%async_computation | async-start | bytes 262144 | tf_op jit(solution)/shard_map/sum_latents/all_to_all | solution.py:792
  36.2 0.0 copy-start.3
  36.2 1.8 %collective-permute-start.11 = (bf16[32,512]{1,0:T(8,128)(2,1)S(1)}, bf16[32,512]{1,0:T(8,128)(2,1)S(1)}, u32[]{:S(2)}, u32[]{:S(2)}) collective-permute-start(bf16[32,512]{1,0:T(8,128)(2,1)S(1)} %add_convert_fusion.m0_ref), channel_id=1, source_target_pairs={{0,1},{1,0},{2,3},{3,2},{4,5},{5,4},{6,7},{7,6},{8,9},{9,8},{10,11... | collective-permute-start | bytes 98312 | tf_op jit(solution)/shard_map/merged_projection/ppermute | solution.py:751
  38.0 1.5 %collective-permute-start.12 = (bf16[32,512]{1,0:T(8,128)(2,1)S(1)}, bf16[32,512]{1,0:T(8,128)(2,1)S(1)}, u32[]{:S(2)}, u32[]{:S(2)}) collective-permute-start(bf16[32,512]{1,0:T(8,128)(2,1)S(1)} %add_convert_fusion.m0_ref), channel_id=1, source_target_pairs={{0,4},{1,5},{2,6},{3,7},{4,0},{5,1},{6,2},{7,3},{8,12},{9,13},{10,... | collective-permute-start | bytes 98312 | tf_op jit(solution)/shard_map/merged_projection/ppermute | solution.py:751
  39.5 0.3 collective-permute-start.13
  40.4 1.7 %collective-permute-done.12.m2_ref = bf16[32,512]{1,0:T(8,128)(2,1)S(1)} collective-permute-done((bf16[32,512]{1,0:T(8,128)(2,1)S(1)}, bf16[32,512]{1,0:T(8,128)(2,1)S(1)}, u32[]{:S(2)}, u32[]{:S(2)}) %collective-permute-start.12) | collective-permute-done | bytes 32800 | tf_op jit(solution)/shard_map/merged_projection/ppermute | solution.py:751
  42.1 2.3 %collective-permute-done.13.m3_ref = bf16[32,512]{1,0:T(8,128)(2,1)S(1)} collective-permute-done((bf16[32,512]{1,0:T(8,128)(2,1)S(1)}, bf16[32,512]{1,0:T(8,128)(2,1)S(1)}, u32[]{:S(2)}, u32[]{:S(2)}) %collective-permute-start.13) | collective-permute-done | bytes 32800 | tf_op jit(solution)/shard_map/merged_projection/ppermute | solution.py:751
  44.4 0.1 share_rows.1
  44.5 0.3 all-to-all-done.p_ref
  44.8 1.6 %tokens.1 = (f32[1,2,2,256]{3,2,1,0:T(2,128)}, bf16[8,8,256]{2,1,0:T(8,128)(2,1)}, bf16[8,8,256]{2,1,0:T(8,128)(2,1)}, bf16[8,8,256]{2,1,0:T(8,128)(2,1)}) custom-call(f32[32,8,128]{2,1,0:T(8,128)S(1)} %all-to-all-done.p_ref, bf16[64,768]{1,0:T(8,128)(2,1)S(1)} %get-tuple-element.27.m_ref, f32[1,768]{1,0:T(1,128)S(1)} %get-tuple-element.28.base_ref, ...), custom_call_target="tpu_custom_call" | custom-call | flops 100000000 | bytes 1000000 | tf_op jit(solution)/shard_map/tokens/pallas_call | solution.py:797
  (17 shorter events, 0.0 us)
Async XLA Ops:
  0.6 22.6 %copy-start = (bf16[27,128,16]{1,2,0:T(8,128)(2,1)S(1)}, bf16[27,128,16]{1,2,0:T(8,128)(2,1)}, u32[]{:S(2)}) copy-start(bf16[27,128,16]{1,2,0:T(8,128)(2,1)} %param.19) | copy-start | bytes 331780
  0.7 5.8 %copy-start.2 = (bf16[1,2,2,16,512]{4,3,2,1,0:T(8,128)(2,1)S(1)}, bf16[1,2,2,16,512]{4,3,2,1,0:T(8,128)(2,1)}, u32[]{:S(2)}) copy-start(bf16[1,2,2,16,512]{4,3,2,1,0:T(8,128)(2,1)} %param.15) | copy-start | bytes 196612
  3.4 17.9 %collective-permute-start.7 = (bf16[64,1920]{1,0:T(8,128)(2,1)}, bf16[64,1920]{1,0:T(8,128)(2,1)S(1)}, u32[]{:S(2)}, u32[]{:S(2)}) collective-permute-start(bf16[64,1920]{1,0:T(8,128)(2,1)} %get-tuple-element.22), channel_id=1, source_target_pairs={{0,1},{1,0},{2,3},{3,2},{4,5},{5,4},{6,7},{7,6},{8,9},{9,8},{10,11... | collective-permute-start | bytes 737288 | tf_op jit(solution)/shard_map/weight_by_group/ppermute | solution.py:699
  6.4 5.6 %collective-permute-start = (bf16[64,512]{1,0:T(8,128)(2,1)S(1)}, bf16[64,512]{1,0:T(8,128)(2,1)S(1)}, u32[]{:S(2)}, u32[]{:S(2)}) collective-permute-start(bf16[64,512]{1,0:T(8,128)(2,1)S(1)} %bitcast.14), channel_id=1, source_target_pairs={{0,24},{2,0},{4,28},{6,4},{8,26},{10,2},{12,30},{14,6},{16,8},{18,... | collective-permute-start | bytes 196616 | tf_op jit(solution)/shard_map/gather_clips/ppermute | solution.py:712
  10.0 5.2 %collective-permute-start.1 = (bf16[64,512]{1,0:T(8,128)(2,1)S(1)}, bf16[64,512]{1,0:T(8,128)(2,1)S(1)}, u32[]{:S(2)}, u32[]{:S(2)}) collective-permute-start(bf16[64,512]{1,0:T(8,128)(2,1)S(1)} %bitcast.15), channel_id=1, source_target_pairs={{0,16},{2,24},{4,20},{6,28},{8,18},{10,26},{12,22},{14,30},{16,0},... | collective-permute-start | bytes 196616 | tf_op jit(solution)/shard_map/gather_clips/ppermute | solution.py:712
  10.0 13.9 %collective-permute-start.8 = (bf16[64,1920]{1,0:T(8,128)(2,1)}, bf16[64,1920]{1,0:T(8,128)(2,1)S(1)}, u32[]{:S(2)}, u32[]{:S(2)}) collective-permute-start(bf16[64,1920]{1,0:T(8,128)(2,1)} %get-tuple-element.23), channel_id=1, source_target_pairs={{0,4},{1,5},{2,6},{3,7},{4,0},{5,1},{6,2},{7,3},{8,12},{9,13},{10,... | collective-permute-start | bytes 737288 | tf_op jit(solution)/shard_map/weight_by_group/ppermute | solution.py:699
  11.5 12.4 %copy-start.1 = (bf16[64,2048]{1,0:T(8,128)(2,1)S(1)}, bf16[64,2048]{1,0:T(8,128)(2,1)}, u32[]{:S(2)}) copy-start(bf16[64,2048]{1,0:T(8,128)(2,1)} %get-tuple-element.21.own_ref) | copy-start | bytes 786436
  11.5 12.4 %collective-permute-start.9 = (bf16[64,1920]{1,0:T(8,128)(2,1)}, bf16[64,1920]{1,0:T(8,128)(2,1)S(1)}, u32[]{:S(2)}, u32[]{:S(2)}) collective-permute-start(bf16[64,1920]{1,0:T(8,128)(2,1)} %get-tuple-element.24), channel_id=1, source_target_pairs={{0,5},{1,4},{2,7},{3,6},{4,1},{5,0},{6,3},{7,2},{8,13},{9,12},{10,... | collective-permute-start | bytes 737288 | tf_op jit(solution)/shard_map/weight_by_group/ppermute | solution.py:699
  12.0 5.3 %collective-permute-start.2 = (bf16[64,512]{1,0:T(8,128)(2,1)S(1)}, bf16[64,512]{1,0:T(8,128)(2,1)S(1)}, u32[]{:S(2)}, u32[]{:S(2)}) collective-permute-start(bf16[64,512]{1,0:T(8,128)(2,1)S(1)} %bitcast.16), channel_id=1, source_target_pairs={{0,8},{2,16},{4,12},{6,20},{8,10},{10,18},{12,14},{14,22},{16,24},... | collective-permute-start | bytes 196616 | tf_op jit(solution)/shard_map/gather_clips/ppermute | solution.py:712
  15.2 4.3 %collective-permute-start.3 = (bf16[64,512]{1,0:T(8,128)(2,1)S(1)}, bf16[64,512]{1,0:T(8,128)(2,1)S(1)}, u32[]{:S(2)}, u32[]{:S(2)}) collective-permute-start(bf16[64,512]{1,0:T(8,128)(2,1)S(1)} %bitcast.17), channel_id=1, source_target_pairs={{0,10},{2,8},{4,14},{6,12},{8,2},{10,0},{12,6},{14,4},{16,26},{18,... | collective-permute-start | bytes 196616 | tf_op jit(solution)/shard_map/gather_clips/ppermute | solution.py:712
  19.6 6.4 %collective-permute-start.4 = (bf16[2,64,512]{2,1,0:T(8,128)(2,1)S(1)}, bf16[2,64,512]{2,1,0:T(8,128)(2,1)S(1)}, u32[]{:S(2)}, u32[]{:S(2)}) collective-permute-start(bf16[2,64,512]{2,1,0:T(8,128)(2,1)S(1)} %get-tuple-element.20), channel_id=1, source_target_pairs={{0,1},{1,0},{2,3},{3,2},{4,5},{5,4},{6,7},{7,6},{8,9},{9,8},{10,11... | collective-permute-start | bytes 393224 | tf_op jit(solution)/shard_map/spread_clips/ppermute | solution.py:727
  19.7 9.4 %collective-permute-start.5 = (bf16[2,64,512]{2,1,0:T(8,128)(2,1)S(1)}, bf16[2,64,512]{2,1,0:T(8,128)(2,1)S(1)}, u32[]{:S(2)}, u32[]{:S(2)}) collective-permute-start(bf16[2,64,512]{2,1,0:T(8,128)(2,1)S(1)} %get-tuple-element.19.refs_0_), channel_id=1, source_target_pairs={{0,4},{1,5},{2,6},{3,7},{4,0},{5,1},{6,2},{7,3},{8,12},{9,13},{10,... | collective-permute-start | bytes 393224 | tf_op jit(solution)/shard_map/spread_clips/ppermute | solution.py:727
  21.3 7.8 %collective-permute-start.6 = (bf16[2,64,512]{2,1,0:T(8,128)(2,1)S(1)}, bf16[2,64,512]{2,1,0:T(8,128)(2,1)S(1)}, u32[]{:S(2)}, u32[]{:S(2)}) collective-permute-start(bf16[2,64,512]{2,1,0:T(8,128)(2,1)S(1)} %get-tuple-element.20), channel_id=1, source_target_pairs={{0,5},{1,4},{2,7},{3,6},{4,1},{5,0},{6,3},{7,2},{8,13},{9,12},{10,... | collective-permute-start | bytes 393224 | tf_op jit(solution)/shard_map/spread_clips/ppermute | solution.py:727
  24.4 4.8 %copy-start.4 = (f32[64,2]{1,0:T(8,128)S(1)}, f32[64,2]{1,0:T(8,128)}, u32[]{:S(2)}) copy-start(f32[64,2]{1,0:T(8,128)} %get-tuple-element.25.scale_ref) | copy-start | bytes 1540
  24.4 4.8 %collective-permute-start.10 = (bf16[992,512]{1,0:T(8,128)(2,1)S(1)}, bf16[992,512]{1,0:T(8,128)(2,1)S(1)}, u32[]{:S(2)}, u32[]{:S(2)}) collective-permute-start(bf16[992,512]{1,0:T(8,128)(2,1)S(1)} %join_weights.1.wt_ref), channel_id=1, source_target_pairs={{0,2},{2,0},{4,6},{6,4},{1,3},{3,1},{5,7},{7,5},{8,10},{10,8},{12,... | collective-permute-start | bytes 3047432 | tf_op jit(solution)/shard_map/join_weights/ppermute | solution.py:744
  32.9 11.9 %all-to-all-start = ((f32[32,8,128]{2,1,0:T(8,128)}), f32[32,8,128]{2,1,0:T(8,128)S(1)}, u32[]{:S(2)}, u32[]{:S(2)}) async-start(f32[32,8,128]{2,1,0:T(8,128)} %convolutions.1), calls=%async_computation | async-start | bytes 262144 | tf_op jit(solution)/shard_map/sum_latents/all_to_all | solution.py:792
  36.2 8.2 %copy-start.3 = (f32[56,128]{1,0:T(8,128)S(1)}, f32[56,128]{1,0:T(8,128)}, u32[]{:S(2)}) copy-start(f32[56,128]{1,0:T(8,128)} %get-tuple-element.26.table_ref) | copy-start | bytes 86020
  36.2 4.2 %collective-permute-start.11 = (bf16[32,512]{1,0:T(8,128)(2,1)S(1)}, bf16[32,512]{1,0:T(8,128)(2,1)S(1)}, u32[]{:S(2)}, u32[]{:S(2)}) collective-permute-start(bf16[32,512]{1,0:T(8,128)(2,1)S(1)} %add_convert_fusion.m0_ref), channel_id=1, source_target_pairs={{0,1},{1,0},{2,3},{3,2},{4,5},{5,4},{6,7},{7,6},{8,9},{9,8},{10,11... | collective-permute-start | bytes 98312 | tf_op jit(solution)/shard_map/merged_projection/ppermute | solution.py:751
  38.0 4.1 %collective-permute-start.12 = (bf16[32,512]{1,0:T(8,128)(2,1)S(1)}, bf16[32,512]{1,0:T(8,128)(2,1)S(1)}, u32[]{:S(2)}, u32[]{:S(2)}) collective-permute-start(bf16[32,512]{1,0:T(8,128)(2,1)S(1)} %add_convert_fusion.m0_ref), channel_id=1, source_target_pairs={{0,4},{1,5},{2,6},{3,7},{4,0},{5,1},{6,2},{7,3},{8,12},{9,13},{10,... | collective-permute-start | bytes 98312 | tf_op jit(solution)/shard_map/merged_projection/ppermute | solution.py:751
  39.5 4.9 %collective-permute-start.13 = (bf16[32,512]{1,0:T(8,128)(2,1)S(1)}, bf16[32,512]{1,0:T(8,128)(2,1)S(1)}, u32[]{:S(2)}, u32[]{:S(2)}) collective-permute-start(bf16[32,512]{1,0:T(8,128)(2,1)S(1)} %add_convert_fusion.m0_ref), channel_id=1, source_target_pairs={{0,5},{1,4},{2,7},{3,6},{4,1},{5,0},{6,3},{7,2},{8,13},{9,12},{10,... | collective-permute-start | bytes 98312 | tf_op jit(solution)/shard_map/merged_projection/ppermute | solution.py:751

commit v2 on v0

--- a/solution.py
+++ b/solution.py
@@ -467,7 +467,7 @@
 def place_kernel(*refs):
     pieces, x_ref = refs[:4], refs[4]
     place = lax.axis_index("tm") // 2 * 4 + lax.axis_index("height")
-    for flip, piece in zip((0, 1, 4, 5), pieces):
+    for flip, piece in zip((0, 5, 4, 1), pieces):
         for core in range(2):
             x_ref[(place ^ flip) + 2 * core] = piece[core]
 
@@ -721,7 +721,7 @@
             name="arrange_clips",
         )(*layers, own)
         pieces = [keep]
-        for flip in (1, 4, 5):
+        for flip in (5, 4, 1):
             pairs = [(i, i ^ flip) for i in range(plane)]
             pieces.append(lax.ppermute(send if flip % 2 else keep, plane_axes, pairs))
     with jax.named_scope("small_weights"):

time: 45.7 us -> 46.1 us (level)
  waiting for transfers between devices: 12.3 us -> 13.7 us
  starting transfers between devices: 23 us -> 22 us
    ppermute x3, waiting for transfers between devices: 2.46 us -> 4.5 us  [grouped(): lax.ppermute(block, plane_axes, [(i, i ^ flip) for i in range(plane)])]
    all_to_all x1, starting transfers between devices: 3.67 us -> 2.97 us  [grouped(): partials = lax.all_to_all(partial, ('dp',) + plane_axes, 0, 0, tiled=True)]
    ppermute x3, waiting for transfers between devices: 3.54 us -> 2.9 us  [grouped(): pieces.append(lax.ppermute(send if flip % 2 else keep, plane_axes, pairs))]
  transfers between devices with their start and end apart: 15 -> 15, of which waited for: 8 -> 7; matrix products, arithmetic and copies ran while one was open for 0% -> 0% of each run, Pallas kernels for 1% -> 1%
where the time goes in v2:
time: 46.1 us; the launch traced here: 45.9 us
  starting transfers between devices  22 us (48%)
  waiting for transfers between devices  13.7 us (30%)
  Pallas kernels  8.59 us (19%)
  between operations  1.42 us (3%)
    ppermute x4, starting transfers between devices, grouped(): layers.append(lax.ppermute(own, ('dp', 'tm'), pairs))  6.88 us
    ppermute x3, starting transfers between devices, grouped(): lax.ppermute(block, plane_axes, [(i, i ^ flip) for i in range(plane)])  5 us
    ppermute x3, waiting for transfers between devices, grouped(): lax.ppermute(block, plane_axes, [(i, i ^ flip) for i in range(plane)])  4.5 us
    ppermute x3, waiting for transfers between devices, grouped(): shares.append(lax.ppermute(share, plane_axes, pairs))  3.99 us
    pallas_call x1, Pallas kernels, grouped(): pl.pallas_call(conv_kernel, out_shape=jax.ShapeDtypeStruct((clips * plane...  3.63 us
    ppermute x3, starting transfers between devices, grouped(): pieces.append(lax.ppermute(send if flip % 2 else keep, plane_axes, pairs))  3.55 us
    ppermute x3, starting transfers between devices, grouped(): shares.append(lax.ppermute(share, plane_axes, pairs))  3.55 us
    all_to_all x1, starting transfers between devices, grouped(): partials = lax.all_to_all(partial, ('dp',) + plane_axes, 0, 0, tiled=True)  2.97 us
  transfers between devices with their start and end apart: 15, of which 7 were waited for; matrix products, arithmetic and copies ran while one was open for 0% of the time, Pallas kernels for 1%

profile of v2, /device:TPU:0, one launch (start us, length us, event | category | flops | bytes accessed | tf_op | source)
XLA Modules:
  0.0 45.9 jit_solution(6931816949660189903)
XLA Ops:
  0.6 0.0 copy-start
  0.7 2.7 %pack_weights.1 = (bf16[64,2048]{1,0:T(8,128)(2,1)}, bf16[64,1920]{1,0:T(8,128)(2,1)}, bf16[64,1920]{1,0:T(8,128)(2,1)}, bf16[64,1920]{1,0:T(8,128)(2,1)}, f32[64,2]{1,0:T(8,128)}, /*index=5*/f32[56,128]{1,0:T(8,128)}) custom-call(f32[1,128]{1,0:T(1,128)} %constant.27.clone.freq_hbm, bf16[1728,128]{1,0:T(8,128)(2,1)} %w_hbm.1, bf16[384,768]{1,0:T(8,128)(2,1)} %qkv_hbm.1, ...), custom_call_target="tpu_custom_call" | custom-call | flops 100000000 | bytes 1000000 | tf_op jit(solution)/shard_map/weight_by_group/pack_weights/pallas_call | solution.py:660
  3.4 3.0 %collective-permute-start.7 = (bf16[64,1920]{1,0:T(8,128)(2,1)}, bf16[64,1920]{1,0:T(8,128)(2,1)S(1)}, u32[]{:S(2)}, u32[]{:S(2)}) collective-permute-start(bf16[64,1920]{1,0:T(8,128)(2,1)} %get-tuple-element.22), channel_id=1, source_target_pairs={{0,1},{1,0},{2,3},{3,2},{4,5},{5,4},{6,7},{7,6},{8,9},{9,8},{10,11... | collective-permute-start | bytes 737288 | tf_op jit(solution)/shard_map/weight_by_group/ppermute | solution.py:699
  6.4 3.6 %collective-permute-start = (bf16[64,512]{1,0:T(8,128)(2,1)S(1)}, bf16[64,512]{1,0:T(8,128)(2,1)S(1)}, u32[]{:S(2)}, u32[]{:S(2)}) collective-permute-start(bf16[64,512]{1,0:T(8,128)(2,1)S(1)} %bitcast.14), channel_id=1, source_target_pairs={{0,24},{2,0},{4,28},{6,4},{8,26},{10,2},{12,30},{14,6},{16,8},{18,... | collective-permute-start | bytes 196616 | tf_op jit(solution)/shard_map/gather_clips/ppermute | solution.py:711
  10.0 1.5 %collective-permute-start.8 = (bf16[64,1920]{1,0:T(8,128)(2,1)}, bf16[64,1920]{1,0:T(8,128)(2,1)S(1)}, u32[]{:S(2)}, u32[]{:S(2)}) collective-permute-start(bf16[64,1920]{1,0:T(8,128)(2,1)} %get-tuple-element.23), channel_id=1, source_target_pairs={{0,4},{1,5},{2,6},{3,7},{4,0},{5,1},{6,2},{7,3},{8,12},{9,13},{10,... | collective-permute-start | bytes 737288 | tf_op jit(solution)/shard_map/weight_by_group/ppermute | solution.py:699
  11.5 0.5 %collective-permute-start.9 = (bf16[64,1920]{1,0:T(8,128)(2,1)}, bf16[64,1920]{1,0:T(8,128)(2,1)S(1)}, u32[]{:S(2)}, u32[]{:S(2)}) collective-permute-start(bf16[64,1920]{1,0:T(8,128)(2,1)} %get-tuple-element.24), channel_id=1, source_target_pairs={{0,5},{1,4},{2,7},{3,6},{4,1},{5,0},{6,3},{7,2},{8,13},{9,12},{10,... | collective-permute-start | bytes 737288 | tf_op jit(solution)/shard_map/weight_by_group/ppermute | solution.py:699
  12.0 2.6 %collective-permute-start.2 = (bf16[64,512]{1,0:T(8,128)(2,1)S(1)}, bf16[64,512]{1,0:T(8,128)(2,1)S(1)}, u32[]{:S(2)}, u32[]{:S(2)}) collective-permute-start(bf16[64,512]{1,0:T(8,128)(2,1)S(1)} %bitcast.16), channel_id=1, source_target_pairs={{0,8},{2,16},{4,12},{6,20},{8,10},{10,18},{12,14},{14,22},{16,24},... | collective-permute-start | bytes 196616 | tf_op jit(solution)/shard_map/gather_clips/ppermute | solution.py:711
  14.7 0.6 %collective-permute-done.1.refs_1_ = bf16[64,512]{1,0:T(8,128)(2,1)S(1)} collective-permute-done((bf16[64,512]{1,0:T(8,128)(2,1)S(1)}, bf16[64,512]{1,0:T(8,128)(2,1)S(1)}, u32[]{:S(2)}, u32[]{:S(2)}) %collective-permute-start.1) | collective-permute-done | bytes 65568 | tf_op jit(solution)/shard_map/gather_clips/ppermute | solution.py:711
  15.2 0.7 %collective-permute-start.3 = (bf16[64,512]{1,0:T(8,128)(2,1)S(1)}, bf16[64,512]{1,0:T(8,128)(2,1)S(1)}, u32[]{:S(2)}, u32[]{:S(2)}) collective-permute-start(bf16[64,512]{1,0:T(8,128)(2,1)S(1)} %bitcast.17), channel_id=1, source_target_pairs={{2,8},{6,12},{8,2},{12,6},{18,24},{22,28},{24,18},{28,22},{3,9},{7... | collective-permute-start | bytes 196616 | tf_op jit(solution)/shard_map/gather_clips/ppermute | solution.py:711
  15.9 1.4 %collective-permute-done.2.refs_2_ = bf16[64,512]{1,0:T(8,128)(2,1)S(1)} collective-permute-done((bf16[64,512]{1,0:T(8,128)(2,1)S(1)}, bf16[64,512]{1,0:T(8,128)(2,1)S(1)}, u32[]{:S(2)}, u32[]{:S(2)}) %collective-permute-start.2) | collective-permute-done | bytes 65568 | tf_op jit(solution)/shard_map/gather_clips/ppermute | solution.py:711
  17.3 0.0 collective-permute-done.3.refs_3_
  17.3 0.1 arrange_clips.1
  17.4 2.5 %collective-permute-start.4 = (bf16[2,64,512]{2,1,0:T(8,128)(2,1)S(1)}, bf16[2,64,512]{2,1,0:T(8,128)(2,1)S(1)}, u32[]{:S(2)}, u32[]{:S(2)}) collective-permute-start(bf16[2,64,512]{2,1,0:T(8,128)(2,1)S(1)} %get-tuple-element.20), channel_id=1, source_target_pairs={{0,5},{1,4},{2,7},{3,6},{4,1},{5,0},{6,3},{7,2},{8,13},{9,12},{10,... | collective-permute-start | bytes 393224 | tf_op jit(solution)/shard_map/spread_clips/ppermute | solution.py:726
  19.9 0.5 %collective-permute-start.5 = (bf16[2,64,512]{2,1,0:T(8,128)(2,1)S(1)}, bf16[2,64,512]{2,1,0:T(8,128)(2,1)S(1)}, u32[]{:S(2)}, u32[]{:S(2)}) collective-permute-start(bf16[2,64,512]{2,1,0:T(8,128)(2,1)S(1)} %get-tuple-element.19.refs_0_), channel_id=1, source_target_pairs={{0,4},{1,5},{2,6},{3,7},{4,0},{5,1},{6,2},{7,3},{8,12},{9,13},{10,... | collective-permute-start | bytes 393224 | tf_op jit(solution)/shard_map/spread_clips/ppermute | solution.py:726
  20.4 0.5 %collective-permute-start.6 = (bf16[2,64,512]{2,1,0:T(8,128)(2,1)S(1)}, bf16[2,64,512]{2,1,0:T(8,128)(2,1)S(1)}, u32[]{:S(2)}, u32[]{:S(2)}) collective-permute-start(bf16[2,64,512]{2,1,0:T(8,128)(2,1)S(1)} %get-tuple-element.20), channel_id=1, source_target_pairs={{0,1},{1,0},{2,3},{3,2},{4,5},{5,4},{6,7},{7,6},{8,9},{9,8},{10,11... | collective-permute-start | bytes 393224 | tf_op jit(solution)/shard_map/spread_clips/ppermute | solution.py:726
  21.0 0.1 constant_dynamic-slice_fusion
  21.1 4.5 %collective-permute-done.8.high_ref = bf16[64,1920]{1,0:T(8,128)(2,1)S(1)} collective-permute-done((bf16[64,1920]{1,0:T(8,128)(2,1)}, bf16[64,1920]{1,0:T(8,128)(2,1)S(1)}, u32[]{:S(2)}, u32[]{:S(2)}) %collective-permute-start.8) | collective-permute-done | bytes 245792 | tf_op jit(solution)/shard_map/weight_by_group/ppermute | solution.py:699
  25.6 0.4 join_weights.1.wt_ref
  26.0 0.0 collective-permute-start.10
  26.0 2.9 %collective-permute-done.5.refs_2_ = bf16[2,64,512]{2,1,0:T(8,128)(2,1)S(1)} collective-permute-done((bf16[2,64,512]{2,1,0:T(8,128)(2,1)S(1)}, bf16[2,64,512]{2,1,0:T(8,128)(2,1)S(1)}, u32[]{:S(2)}, u32[]{:S(2)}) %collective-permute-start.5) | collective-permute-done | bytes 131104 | tf_op jit(solution)/shard_map/spread_clips/ppermute | solution.py:726
  28.9 0.1 place_clip.1.x_ref
  29.0 3.6 %convolutions.1 = f32[32,8,128]{2,1,0:T(8,128)} custom-call(bf16[8,64,512]{2,1,0:T(8,128)(2,1)S(1)} %place_clip.1.x_ref, bf16[992,512]{1,0:T(8,128)(2,1)S(1)} %join_weights.1.wt_ref, bf16[992,512]{1,0:T(8,128)(2,1)S(1)} %collective-permute-done.10.pair_ref, f32[64,2]{1,0:T(8,128)S(1)} %copy-done.4, bf16[432,64]{1,0:T(8,128)(2,1)S(1)} %bitcast.13), custom_call_target="tpu_custom_call" | custom-call | flops 1006632960 | bytes 1000000 | tf_op jit(solution)/shard_map/convolutions/pallas_call | solution.py:777
  32.6 3.0 %all-to-all-start = ((f32[32,8,128]{2,1,0:T(8,128)}), f32[32,8,128]{2,1,0:T(8,128)S(1)}, u32[]{:S(2)}, u32[]{:S(2)}) async-start(f32[32,8,128]{2,1,0:T(8,128)} %convolutions.1), calls=%async_computation | async-start | bytes 262144 | tf_op jit(solution)/shard_map/sum_latents/all_to_all | solution.py:791
  35.6 0.0 copy-start.3
  35.7 1.8 %collective-permute-start.11 = (bf16[32,512]{1,0:T(8,128)(2,1)S(1)}, bf16[32,512]{1,0:T(8,128)(2,1)S(1)}, u32[]{:S(2)}, u32[]{:S(2)}) collective-permute-start(bf16[32,512]{1,0:T(8,128)(2,1)S(1)} %add_convert_fusion.m0_ref), channel_id=1, source_target_pairs={{0,1},{1,0},{2,3},{3,2},{4,5},{5,4},{6,7},{7,6},{8,9},{9,8},{10,11... | collective-permute-start | bytes 98312 | tf_op jit(solution)/shard_map/merged_projection/ppermute | solution.py:750
  37.5 1.5 %collective-permute-start.12 = (bf16[32,512]{1,0:T(8,128)(2,1)S(1)}, bf16[32,512]{1,0:T(8,128)(2,1)S(1)}, u32[]{:S(2)}, u32[]{:S(2)}) collective-permute-start(bf16[32,512]{1,0:T(8,128)(2,1)S(1)} %add_convert_fusion.m0_ref), channel_id=1, source_target_pairs={{0,4},{1,5},{2,6},{3,7},{4,0},{5,1},{6,2},{7,3},{8,12},{9,13},{10,... | collective-permute-start | bytes 98312 | tf_op jit(solution)/shard_map/merged_projection/ppermute | solution.py:750
  39.0 0.3 collective-permute-start.13
  39.9 1.7 %collective-permute-done.12.m2_ref = bf16[32,512]{1,0:T(8,128)(2,1)S(1)} collective-permute-done((bf16[32,512]{1,0:T(8,128)(2,1)S(1)}, bf16[32,512]{1,0:T(8,128)(2,1)S(1)}, u32[]{:S(2)}, u32[]{:S(2)}) %collective-permute-start.12) | collective-permute-done | bytes 32800 | tf_op jit(solution)/shard_map/merged_projection/ppermute | solution.py:750
  41.6 2.3 %collective-permute-done.13.m3_ref = bf16[32,512]{1,0:T(8,128)(2,1)S(1)} collective-permute-done((bf16[32,512]{1,0:T(8,128)(2,1)S(1)}, bf16[32,512]{1,0:T(8,128)(2,1)S(1)}, u32[]{:S(2)}, u32[]{:S(2)}) %collective-permute-start.13) | collective-permute-done | bytes 32800 | tf_op jit(solution)/shard_map/merged_projection/ppermute | solution.py:750
  43.9 0.1 share_rows.1
  43.9 0.3 all-to-all-done.p_ref
  44.3 1.6 %tokens.1 = (f32[1,2,2,256]{3,2,1,0:T(2,128)}, bf16[8,8,256]{2,1,0:T(8,128)(2,1)}, bf16[8,8,256]{2,1,0:T(8,128)(2,1)}, bf16[8,8,256]{2,1,0:T(8,128)(2,1)}) custom-call(f32[32,8,128]{2,1,0:T(8,128)S(1)} %all-to-all-done.p_ref, bf16[64,768]{1,0:T(8,128)(2,1)S(1)} %get-tuple-element.27.m_ref, f32[1,768]{1,0:T(1,128)S(1)} %get-tuple-element.28.base_ref, ...), custom_call_target="tpu_custom_call" | custom-call | flops 100000000 | bytes 1000000 | tf_op jit(solution)/shard_map/tokens/pallas_call | solution.py:796
  (17 shorter events, 0.0 us)
Async XLA Ops:
  0.6 20.3 %copy-start = (bf16[27,128,16]{1,2,0:T(8,128)(2,1)S(1)}, bf16[27,128,16]{1,2,0:T(8,128)(2,1)}, u32[]{:S(2)}) copy-start(bf16[27,128,16]{1,2,0:T(8,128)(2,1)} %param.19) | copy-start | bytes 331780
  0.7 5.8 %copy-start.2 = (bf16[1,2,2,16,512]{4,3,2,1,0:T(8,128)(2,1)S(1)}, bf16[1,2,2,16,512]{4,3,2,1,0:T(8,128)(2,1)}, u32[]{:S(2)}) copy-start(bf16[1,2,2,16,512]{4,3,2,1,0:T(8,128)(2,1)} %param.15) | copy-start | bytes 196612
  3.4 17.0 %collective-permute-start.7 = (bf16[64,1920]{1,0:T(8,128)(2,1)}, bf16[64,1920]{1,0:T(8,128)(2,1)S(1)}, u32[]{:S(2)}, u32[]{:S(2)}) collective-permute-start(bf16[64,1920]{1,0:T(8,128)(2,1)} %get-tuple-element.22), channel_id=1, source_target_pairs={{0,1},{1,0},{2,3},{3,2},{4,5},{5,4},{6,7},{7,6},{8,9},{9,8},{10,11... | collective-permute-start | bytes 737288 | tf_op jit(solution)/shard_map/weight_by_group/ppermute | solution.py:699
  6.4 5.6 %collective-permute-start = (bf16[64,512]{1,0:T(8,128)(2,1)S(1)}, bf16[64,512]{1,0:T(8,128)(2,1)S(1)}, u32[]{:S(2)}, u32[]{:S(2)}) collective-permute-start(bf16[64,512]{1,0:T(8,128)(2,1)S(1)} %bitcast.14), channel_id=1, source_target_pairs={{0,24},{2,0},{4,28},{6,4},{8,26},{10,2},{12,30},{14,6},{16,8},{18,... | collective-permute-start | bytes 196616 | tf_op jit(solution)/shard_map/gather_clips/ppermute | solution.py:711
  10.0 5.2 %collective-permute-start.1 = (bf16[64,512]{1,0:T(8,128)(2,1)S(1)}, bf16[64,512]{1,0:T(8,128)(2,1)S(1)}, u32[]{:S(2)}, u32[]{:S(2)}) collective-permute-start(bf16[64,512]{1,0:T(8,128)(2,1)S(1)} %bitcast.15), channel_id=1, source_target_pairs={{0,16},{2,24},{4,20},{6,28},{8,18},{10,26},{12,22},{14,30},{16,0},... | collective-permute-start | bytes 196616 | tf_op jit(solution)/shard_map/gather_clips/ppermute | solution.py:711
  10.0 15.5 %collective-permute-start.8 = (bf16[64,1920]{1,0:T(8,128)(2,1)}, bf16[64,1920]{1,0:T(8,128)(2,1)S(1)}, u32[]{:S(2)}, u32[]{:S(2)}) collective-permute-start(bf16[64,1920]{1,0:T(8,128)(2,1)} %get-tuple-element.23), channel_id=1, source_target_pairs={{0,4},{1,5},{2,6},{3,7},{4,0},{5,1},{6,2},{7,3},{8,12},{9,13},{10,... | collective-permute-start | bytes 737288 | tf_op jit(solution)/shard_map/weight_by_group/ppermute | solution.py:699
  11.5 14.0 %copy-start.1 = (bf16[64,2048]{1,0:T(8,128)(2,1)S(1)}, bf16[64,2048]{1,0:T(8,128)(2,1)}, u32[]{:S(2)}) copy-start(bf16[64,2048]{1,0:T(8,128)(2,1)} %get-tuple-element.21.own_ref) | copy-start | bytes 786436
  11.5 14.0 %collective-permute-start.9 = (bf16[64,1920]{1,0:T(8,128)(2,1)}, bf16[64,1920]{1,0:T(8,128)(2,1)S(1)}, u32[]{:S(2)}, u32[]{:S(2)}) collective-permute-start(bf16[64,1920]{1,0:T(8,128)(2,1)} %get-tuple-element.24), channel_id=1, source_target_pairs={{0,5},{1,4},{2,7},{3,6},{4,1},{5,0},{6,3},{7,2},{8,13},{9,12},{10,... | collective-permute-start | bytes 737288 | tf_op jit(solution)/shard_map/weight_by_group/ppermute | solution.py:699
  12.0 5.3 %collective-permute-start.2 = (bf16[64,512]{1,0:T(8,128)(2,1)S(1)}, bf16[64,512]{1,0:T(8,128)(2,1)S(1)}, u32[]{:S(2)}, u32[]{:S(2)}) collective-permute-start(bf16[64,512]{1,0:T(8,128)(2,1)S(1)} %bitcast.16), channel_id=1, source_target_pairs={{0,8},{2,16},{4,12},{6,20},{8,10},{10,18},{12,14},{14,22},{16,24},... | collective-permute-start | bytes 196616 | tf_op jit(solution)/shard_map/gather_clips/ppermute | solution.py:711
  15.2 2.1 %collective-permute-start.3 = (bf16[64,512]{1,0:T(8,128)(2,1)S(1)}, bf16[64,512]{1,0:T(8,128)(2,1)S(1)}, u32[]{:S(2)}, u32[]{:S(2)}) collective-permute-start(bf16[64,512]{1,0:T(8,128)(2,1)S(1)} %bitcast.17), channel_id=1, source_target_pairs={{2,8},{6,12},{8,2},{12,6},{18,24},{22,28},{24,18},{28,22},{3,9},{7... | collective-permute-start | bytes 196616 | tf_op jit(solution)/shard_map/gather_clips/ppermute | solution.py:711
  17.4 8.6 %collective-permute-start.4 = (bf16[2,64,512]{2,1,0:T(8,128)(2,1)S(1)}, bf16[2,64,512]{2,1,0:T(8,128)(2,1)S(1)}, u32[]{:S(2)}, u32[]{:S(2)}) collective-permute-start(bf16[2,64,512]{2,1,0:T(8,128)(2,1)S(1)} %get-tuple-element.20), channel_id=1, source_target_pairs={{0,5},{1,4},{2,7},{3,6},{4,1},{5,0},{6,3},{7,2},{8,13},{9,12},{10,... | collective-permute-start | bytes 393224 | tf_op jit(solution)/shard_map/spread_clips/ppermute | solution.py:726
  19.9 9.0 %collective-permute-start.5 = (bf16[2,64,512]{2,1,0:T(8,128)(2,1)S(1)}, bf16[2,64,512]{2,1,0:T(8,128)(2,1)S(1)}, u32[]{:S(2)}, u32[]{:S(2)}) collective-permute-start(bf16[2,64,512]{2,1,0:T(8,128)(2,1)S(1)} %get-tuple-element.19.refs_0_), channel_id=1, source_target_pairs={{0,4},{1,5},{2,6},{3,7},{4,0},{5,1},{6,2},{7,3},{8,12},{9,13},{10,... | collective-permute-start | bytes 393224 | tf_op jit(solution)/shard_map/spread_clips/ppermute | solution.py:726
  20.4 8.5 %collective-permute-start.6 = (bf16[2,64,512]{2,1,0:T(8,128)(2,1)S(1)}, bf16[2,64,512]{2,1,0:T(8,128)(2,1)S(1)}, u32[]{:S(2)}, u32[]{:S(2)}) collective-permute-start(bf16[2,64,512]{2,1,0:T(8,128)(2,1)S(1)} %get-tuple-element.20), channel_id=1, source_target_pairs={{0,1},{1,0},{2,3},{3,2},{4,5},{5,4},{6,7},{7,6},{8,9},{9,8},{10,11... | collective-permute-start | bytes 393224 | tf_op jit(solution)/shard_map/spread_clips/ppermute | solution.py:726
  26.0 3.0 %copy-start.4 = (f32[64,2]{1,0:T(8,128)S(1)}, f32[64,2]{1,0:T(8,128)}, u32[]{:S(2)}) copy-start(f32[64,2]{1,0:T(8,128)} %get-tuple-element.25.scale_ref) | copy-start | bytes 1540
  26.0 3.0 %collective-permute-start.10 = (bf16[992,512]{1,0:T(8,128)(2,1)S(1)}, bf16[992,512]{1,0:T(8,128)(2,1)S(1)}, u32[]{:S(2)}, u32[]{:S(2)}) collective-permute-start(bf16[992,512]{1,0:T(8,128)(2,1)S(1)} %join_weights.1.wt_ref), channel_id=1, source_target_pairs={{0,2},{2,0},{4,6},{6,4},{1,3},{3,1},{5,7},{7,5},{8,10},{10,8},{12,... | collective-permute-start | bytes 3047432 | tf_op jit(solution)/shard_map/join_weights/ppermute | solution.py:743
  32.6 11.6 %all-to-all-start = ((f32[32,8,128]{2,1,0:T(8,128)}), f32[32,8,128]{2,1,0:T(8,128)S(1)}, u32[]{:S(2)}, u32[]{:S(2)}) async-start(f32[32,8,128]{2,1,0:T(8,128)} %convolutions.1), calls=%async_computation | async-start | bytes 262144 | tf_op jit(solution)/shard_map/sum_latents/all_to_all | solution.py:791
  35.6 8.2 %copy-start.3 = (f32[56,128]{1,0:T(8,128)S(1)}, f32[56,128]{1,0:T(8,128)}, u32[]{:S(2)}) copy-start(f32[56,128]{1,0:T(8,128)} %get-tuple-element.26.table_ref) | copy-start | bytes 86020
  35.7 4.2 %collective-permute-start.11 = (bf16[32,512]{1,0:T(8,128)(2,1)S(1)}, bf16[32,512]{1,0:T(8,128)(2,1)S(1)}, u32[]{:S(2)}, u32[]{:S(2)}) collective-permute-start(bf16[32,512]{1,0:T(8,128)(2,1)S(1)} %add_convert_fusion.m0_ref), channel_id=1, source_target_pairs={{0,1},{1,0},{2,3},{3,2},{4,5},{5,4},{6,7},{7,6},{8,9},{9,8},{10,11... | collective-permute-start | bytes 98312 | tf_op jit(solution)/shard_map/merged_projection/ppermute | solution.py:750
  37.5 4.1 %collective-permute-start.12 = (bf16[32,512]{1,0:T(8,128)(2,1)S(1)}, bf16[32,512]{1,0:T(8,128)(2,1)S(1)}, u32[]{:S(2)}, u32[]{:S(2)}) collective-permute-start(bf16[32,512]{1,0:T(8,128)(2,1)S(1)} %add_convert_fusion.m0_ref), channel_id=1, source_target_pairs={{0,4},{1,5},{2,6},{3,7},{4,0},{5,1},{6,2},{7,3},{8,12},{9,13},{10,... | collective-permute-start | bytes 98312 | tf_op jit(solution)/shard_map/merged_projection/ppermute | solution.py:750
  39.0 4.9 %collective-permute-start.13 = (bf16[32,512]{1,0:T(8,128)(2,1)S(1)}, bf16[32,512]{1,0:T(8,128)(2,1)S(1)}, u32[]{:S(2)}, u32[]{:S(2)}) collective-permute-start(bf16[32,512]{1,0:T(8,128)(2,1)S(1)} %add_convert_fusion.m0_ref), channel_id=1, source_target_pairs={{0,5},{1,4},{2,7},{3,6},{4,1},{5,0},{6,3},{7,2},{8,13},{9,12},{10,... | collective-permute-start | bytes 98312 | tf_op jit(solution)/shard_map/merged_projection/ppermute | solution.py:750

commit v3 on v0

--- a/solution.py
+++ b/solution.py
@@ -419,7 +419,7 @@
     return taps
 
 
-def join_kernel(own_ref, side_ref, high_ref, far_ref, wt_ref, all_ref):
+def join_kernel(own_ref, far_ref, high_ref, side_ref, wt_ref, all_ref):
     channels, width = side_ref.shape
     inner = wt_ref.shape[1]
     depth = TAPS * inner // 8
@@ -695,7 +695,7 @@
             *small_arrays,
         )
         blocks = [packed[0]]
-        for flip, block in zip((1, 4, 5), packed[1:]):
+        for flip, block in zip((5, 4, 1), packed[:0:-1]):
             blocks.append(lax.ppermute(block, plane_axes, [(i, i ^ flip) for i in range(plane)]))
     with jax.named_scope("gather_clips"):
         own = clip_inputs.reshape(64, channels)

time: 45.7 us -> 46.4 us (1.015)
  starting transfers between devices: 23 us -> 25.5 us
  waiting for transfers between devices: 12.3 us -> 10.5 us
    ppermute x3, waiting for transfers between devices: 2.46 us -> 0.01 us  [grouped(): lax.ppermute(block, plane_axes, [(i, i ^ flip) for i in range(plane)])]
    ppermute x1, starting transfers between devices: 0.36 us -> 1.84 us  [grouped(): joined_pair = lax.ppermute(joined, 'tm', [(i, i ^ 1) for i in range(steps)])]
    all_to_all x1, starting transfers between devices: 3.67 us -> 4.64 us  [grouped(): partials = lax.all_to_all(partial, ('dp',) + plane_axes, 0, 0, tiled=True)]
    ppermute x4, waiting for transfers between devices: 2.01 us -> 2.65 us  [grouped(): layers.append(lax.ppermute(own, ('dp', 'tm'), pairs))]
  transfers between devices with their start and end apart: 15 -> 15, of which waited for: 8 -> 7; matrix products, arithmetic and copies ran while one was open for 0% -> 0% of each run, Pallas kernels for 1% -> 1%
where the time goes in v3:
time: 46.4 us; the launch traced here: 46.1 us
  starting transfers between devices  25.5 us (55%)
  waiting for transfers between devices  10.5 us (23%)
  Pallas kernels  8.6 us (19%)
  between operations  1.43 us (3%)
    ppermute x4, starting transfers between devices, grouped(): layers.append(lax.ppermute(own, ('dp', 'tm'), pairs))  6.89 us
    ppermute x3, starting transfers between devices, grouped(): lax.ppermute(block, plane_axes, [(i, i ^ flip) for i in range(plane)])  5 us
    all_to_all x1, starting transfers between devices, grouped(): partials = lax.all_to_all(partial, ('dp',) + plane_axes, 0, 0, tiled=True)  4.64 us
    ppermute x3, waiting for transfers between devices, grouped(): shares.append(lax.ppermute(share, plane_axes, pairs))  3.99 us
    pallas_call x1, Pallas kernels, grouped(): pl.pallas_call(conv_kernel, out_shape=jax.ShapeDtypeStruct((clips * plane...  3.64 us
    ppermute x3, starting transfers between devices, grouped(): pieces.append(lax.ppermute(send if flip % 2 else keep, plane_axes, pairs))  3.55 us
    ppermute x3, starting transfers between devices, grouped(): shares.append(lax.ppermute(share, plane_axes, pairs))  3.55 us
    ppermute x3, waiting for transfers between devices, grouped(): pieces.append(lax.ppermute(send if flip % 2 else keep, plane_axes, pairs))  3.52 us
  transfers between devices with their start and end apart: 15, of which 7 were waited for; matrix products, arithmetic and copies ran while one was open for 0% of the time, Pallas kernels for 1%

profile of v3, /device:TPU:0, one launch (start us, length us, event | category | flops | bytes accessed | tf_op | source)
XLA Modules:
  0.0 46.1 jit_solution(15630434373820668539)
XLA Ops:
  0.6 0.0 copy-start
  0.7 2.7 %pack_weights.1 = (bf16[64,2048]{1,0:T(8,128)(2,1)}, bf16[64,1920]{1,0:T(8,128)(2,1)}, bf16[64,1920]{1,0:T(8,128)(2,1)}, bf16[64,1920]{1,0:T(8,128)(2,1)}, f32[64,2]{1,0:T(8,128)}, /*index=5*/f32[56,128]{1,0:T(8,128)}) custom-call(f32[1,128]{1,0:T(1,128)} %constant.27.clone.freq_hbm, bf16[1728,128]{1,0:T(8,128)(2,1)} %w_hbm.1, bf16[384,768]{1,0:T(8,128)(2,1)} %qkv_hbm.1, ...), custom_call_target="tpu_custom_call" | custom-call | flops 100000000 | bytes 1000000 | tf_op jit(solution)/shard_map/weight_by_group/pack_weights/pallas_call | solution.py:660
  3.4 4.0 %collective-permute-start.7 = (bf16[64,1920]{1,0:T(8,128)(2,1)}, bf16[64,1920]{1,0:T(8,128)(2,1)S(1)}, u32[]{:S(2)}, u32[]{:S(2)}) collective-permute-start(bf16[64,1920]{1,0:T(8,128)(2,1)} %get-tuple-element.22), channel_id=1, source_target_pairs={{0,5},{1,4},{2,7},{3,6},{4,1},{5,0},{6,3},{7,2},{8,13},{9,12},{10,... | collective-permute-start | bytes 737288 | tf_op jit(solution)/shard_map/weight_by_group/ppermute | solution.py:699
  7.4 3.6 %collective-permute-start = (bf16[64,512]{1,0:T(8,128)(2,1)S(1)}, bf16[64,512]{1,0:T(8,128)(2,1)S(1)}, u32[]{:S(2)}, u32[]{:S(2)}) collective-permute-start(bf16[64,512]{1,0:T(8,128)(2,1)S(1)} %bitcast.14), channel_id=1, source_target_pairs={{0,24},{2,0},{4,28},{6,4},{8,26},{10,2},{12,30},{14,6},{16,8},{18,... | collective-permute-start | bytes 196616 | tf_op jit(solution)/shard_map/gather_clips/ppermute | solution.py:711
  11.0 0.5 %collective-permute-start.8 = (bf16[64,1920]{1,0:T(8,128)(2,1)}, bf16[64,1920]{1,0:T(8,128)(2,1)S(1)}, u32[]{:S(2)}, u32[]{:S(2)}) collective-permute-start(bf16[64,1920]{1,0:T(8,128)(2,1)} %get-tuple-element.23), channel_id=1, source_target_pairs={{0,4},{1,5},{2,6},{3,7},{4,0},{5,1},{6,2},{7,3},{8,12},{9,13},{10,... | collective-permute-start | bytes 737288 | tf_op jit(solution)/shard_map/weight_by_group/ppermute | solution.py:699
  11.5 0.5 %collective-permute-start.9 = (bf16[64,1920]{1,0:T(8,128)(2,1)}, bf16[64,1920]{1,0:T(8,128)(2,1)S(1)}, u32[]{:S(2)}, u32[]{:S(2)}) collective-permute-start(bf16[64,1920]{1,0:T(8,128)(2,1)} %get-tuple-element.24), channel_id=1, source_target_pairs={{0,1},{1,0},{2,3},{3,2},{4,5},{5,4},{6,7},{7,6},{8,9},{9,8},{10,11... | collective-permute-start | bytes 737288 | tf_op jit(solution)/shard_map/weight_by_group/ppermute | solution.py:699
  12.0 0.9 %collective-permute-done.refs_0_ = bf16[64,512]{1,0:T(8,128)(2,1)S(1)} collective-permute-done((bf16[64,512]{1,0:T(8,128)(2,1)S(1)}, bf16[64,512]{1,0:T(8,128)(2,1)S(1)}, u32[]{:S(2)}, u32[]{:S(2)}) %collective-permute-start) | collective-permute-done | bytes 65568 | tf_op jit(solution)/shard_map/gather_clips/ppermute | solution.py:711
  13.0 2.6 %collective-permute-start.2 = (bf16[64,512]{1,0:T(8,128)(2,1)S(1)}, bf16[64,512]{1,0:T(8,128)(2,1)S(1)}, u32[]{:S(2)}, u32[]{:S(2)}) collective-permute-start(bf16[64,512]{1,0:T(8,128)(2,1)S(1)} %bitcast.16), channel_id=1, source_target_pairs={{0,8},{2,16},{4,12},{6,20},{8,10},{10,18},{12,14},{14,22},{16,24},... | collective-permute-start | bytes 196616 | tf_op jit(solution)/shard_map/gather_clips/ppermute | solution.py:711
  15.6 0.6 %collective-permute-done.1.refs_1_ = bf16[64,512]{1,0:T(8,128)(2,1)S(1)} collective-permute-done((bf16[64,512]{1,0:T(8,128)(2,1)S(1)}, bf16[64,512]{1,0:T(8,128)(2,1)S(1)}, u32[]{:S(2)}, u32[]{:S(2)}) %collective-permute-start.1) | collective-permute-done | bytes 65568 | tf_op jit(solution)/shard_map/gather_clips/ppermute | solution.py:711
  16.2 0.7 %collective-permute-start.3 = (bf16[64,512]{1,0:T(8,128)(2,1)S(1)}, bf16[64,512]{1,0:T(8,128)(2,1)S(1)}, u32[]{:S(2)}, u32[]{:S(2)}) collective-permute-start(bf16[64,512]{1,0:T(8,128)(2,1)S(1)} %bitcast.17), channel_id=1, source_target_pairs={{2,8},{6,12},{8,2},{12,6},{18,24},{22,28},{24,18},{28,22},{3,9},{7... | collective-permute-start | bytes 196616 | tf_op jit(solution)/shard_map/gather_clips/ppermute | solution.py:711
  16.8 1.1 %collective-permute-done.2.refs_2_ = bf16[64,512]{1,0:T(8,128)(2,1)S(1)} collective-permute-done((bf16[64,512]{1,0:T(8,128)(2,1)S(1)}, bf16[64,512]{1,0:T(8,128)(2,1)S(1)}, u32[]{:S(2)}, u32[]{:S(2)}) %collective-permute-start.2) | collective-permute-done | bytes 65568 | tf_op jit(solution)/shard_map/gather_clips/ppermute | solution.py:711
  18.0 0.1 arrange_clips.1
  18.0 0.9 %collective-permute-start.4 = (bf16[2,64,512]{2,1,0:T(8,128)(2,1)S(1)}, bf16[2,64,512]{2,1,0:T(8,128)(2,1)S(1)}, u32[]{:S(2)}, u32[]{:S(2)}) collective-permute-start(bf16[2,64,512]{2,1,0:T(8,128)(2,1)S(1)} %get-tuple-element.20), channel_id=1, source_target_pairs={{0,1},{1,0},{2,3},{3,2},{4,5},{5,4},{6,7},{7,6},{8,9},{9,8},{10,11... | collective-permute-start | bytes 393224 | tf_op jit(solution)/shard_map/spread_clips/ppermute | solution.py:726
  19.0 1.5 %collective-permute-start.5 = (bf16[2,64,512]{2,1,0:T(8,128)(2,1)S(1)}, bf16[2,64,512]{2,1,0:T(8,128)(2,1)S(1)}, u32[]{:S(2)}, u32[]{:S(2)}) collective-permute-start(bf16[2,64,512]{2,1,0:T(8,128)(2,1)S(1)} %get-tuple-element.19.refs_0_), channel_id=1, source_target_pairs={{0,4},{1,5},{2,6},{3,7},{4,0},{5,1},{6,2},{7,3},{8,12},{9,13},{10,... | collective-permute-start | bytes 393224 | tf_op jit(solution)/shard_map/spread_clips/ppermute | solution.py:726
  20.5 1.1 %collective-permute-start.6 = (bf16[2,64,512]{2,1,0:T(8,128)(2,1)S(1)}, bf16[2,64,512]{2,1,0:T(8,128)(2,1)S(1)}, u32[]{:S(2)}, u32[]{:S(2)}) collective-permute-start(bf16[2,64,512]{2,1,0:T(8,128)(2,1)S(1)} %get-tuple-element.20), channel_id=1, source_target_pairs={{0,5},{1,4},{2,7},{3,6},{4,1},{5,0},{6,3},{7,2},{8,13},{9,12},{10,... | collective-permute-start | bytes 393224 | tf_op jit(solution)/shard_map/spread_clips/ppermute | solution.py:726
  21.6 0.1 constant_dynamic-slice_fusion
  21.7 0.0 collective-permute-done.8.high_ref
  21.7 0.4 join_weights.1.wt_ref
  22.2 1.8 %collective-permute-start.10 = (bf16[992,512]{1,0:T(8,128)(2,1)S(1)}, bf16[992,512]{1,0:T(8,128)(2,1)S(1)}, u32[]{:S(2)}, u32[]{:S(2)}) collective-permute-start(bf16[992,512]{1,0:T(8,128)(2,1)S(1)} %join_weights.1.wt_ref), channel_id=1, source_target_pairs={{0,2},{2,0},{4,6},{6,4},{1,3},{3,1},{5,7},{7,5},{8,10},{10,8},{12,... | collective-permute-start | bytes 3047432 | tf_op jit(solution)/shard_map/join_weights/ppermute | solution.py:743
  24.0 3.5 %collective-permute-done.6.refs_3_ = bf16[2,64,512]{2,1,0:T(8,128)(2,1)S(1)} collective-permute-done((bf16[2,64,512]{2,1,0:T(8,128)(2,1)S(1)}, bf16[2,64,512]{2,1,0:T(8,128)(2,1)S(1)}, u32[]{:S(2)}, u32[]{:S(2)}) %collective-permute-start.6) | collective-permute-done | bytes 131104 | tf_op jit(solution)/shard_map/spread_clips/ppermute | solution.py:726
  27.5 0.1 place_clip.1.x_ref
  27.6 3.6 %convolutions.1 = f32[32,8,128]{2,1,0:T(8,128)} custom-call(bf16[8,64,512]{2,1,0:T(8,128)(2,1)S(1)} %place_clip.1.x_ref, bf16[992,512]{1,0:T(8,128)(2,1)S(1)} %join_weights.1.wt_ref, bf16[992,512]{1,0:T(8,128)(2,1)S(1)} %collective-permute-done.10.pair_ref, f32[64,2]{1,0:T(8,128)S(1)} %copy-done.4, bf16[432,64]{1,0:T(8,128)(2,1)S(1)} %bitcast.13), custom_call_target="tpu_custom_call" | custom-call | flops 1006632960 | bytes 1000000 | tf_op jit(solution)/shard_map/convolutions/pallas_call | solution.py:777
  31.3 4.6 %all-to-all-start = ((f32[32,8,128]{2,1,0:T(8,128)}), f32[32,8,128]{2,1,0:T(8,128)S(1)}, u32[]{:S(2)}, u32[]{:S(2)}) async-start(f32[32,8,128]{2,1,0:T(8,128)} %convolutions.1), calls=%async_computation | async-start | bytes 262144 | tf_op jit(solution)/shard_map/sum_latents/all_to_all | solution.py:791
  35.9 0.0 copy-start.3
  35.9 1.8 %collective-permute-start.11 = (bf16[32,512]{1,0:T(8,128)(2,1)S(1)}, bf16[32,512]{1,0:T(8,128)(2,1)S(1)}, u32[]{:S(2)}, u32[]{:S(2)}) collective-permute-start(bf16[32,512]{1,0:T(8,128)(2,1)S(1)} %add_convert_fusion.m0_ref), channel_id=1, source_target_pairs={{0,1},{1,0},{2,3},{3,2},{4,5},{5,4},{6,7},{7,6},{8,9},{9,8},{10,11... | collective-permute-start | bytes 98312 | tf_op jit(solution)/shard_map/merged_projection/ppermute | solution.py:750
  37.8 1.5 %collective-permute-start.12 = (bf16[32,512]{1,0:T(8,128)(2,1)S(1)}, bf16[32,512]{1,0:T(8,128)(2,1)S(1)}, u32[]{:S(2)}, u32[]{:S(2)}) collective-permute-start(bf16[32,512]{1,0:T(8,128)(2,1)S(1)} %add_convert_fusion.m0_ref), channel_id=1, source_target_pairs={{0,4},{1,5},{2,6},{3,7},{4,0},{5,1},{6,2},{7,3},{8,12},{9,13},{10,... | collective-permute-start | bytes 98312 | tf_op jit(solution)/shard_map/merged_projection/ppermute | solution.py:750
  39.2 0.3 collective-permute-start.13
  40.2 1.7 %collective-permute-done.12.m2_ref = bf16[32,512]{1,0:T(8,128)(2,1)S(1)} collective-permute-done((bf16[32,512]{1,0:T(8,128)(2,1)S(1)}, bf16[32,512]{1,0:T(8,128)(2,1)S(1)}, u32[]{:S(2)}, u32[]{:S(2)}) %collective-permute-start.12) | collective-permute-done | bytes 32800 | tf_op jit(solution)/shard_map/merged_projection/ppermute | solution.py:750
  41.9 2.3 %collective-permute-done.13.m3_ref = bf16[32,512]{1,0:T(8,128)(2,1)S(1)} collective-permute-done((bf16[32,512]{1,0:T(8,128)(2,1)S(1)}, bf16[32,512]{1,0:T(8,128)(2,1)S(1)}, u32[]{:S(2)}, u32[]{:S(2)}) %collective-permute-start.13) | collective-permute-done | bytes 32800 | tf_op jit(solution)/shard_map/merged_projection/ppermute | solution.py:750
  44.1 0.1 share_rows.1
  44.2 0.3 all-to-all-done.p_ref
  44.5 1.6 %tokens.1 = (f32[1,2,2,256]{3,2,1,0:T(2,128)}, bf16[8,8,256]{2,1,0:T(8,128)(2,1)}, bf16[8,8,256]{2,1,0:T(8,128)(2,1)}, bf16[8,8,256]{2,1,0:T(8,128)(2,1)}) custom-call(f32[32,8,128]{2,1,0:T(8,128)S(1)} %all-to-all-done.p_ref, bf16[64,768]{1,0:T(8,128)(2,1)S(1)} %get-tuple-element.27.m_ref, f32[1,768]{1,0:T(1,128)S(1)} %get-tuple-element.28.base_ref, ...), custom_call_target="tpu_custom_call" | custom-call | flops 100000000 | bytes 1000000 | tf_op jit(solution)/shard_map/tokens/pallas_call | solution.py:796
  (17 shorter events, 0.0 us)
Async XLA Ops:
  0.6 21.0 %copy-start = (bf16[27,128,16]{1,2,0:T(8,128)(2,1)S(1)}, bf16[27,128,16]{1,2,0:T(8,128)(2,1)}, u32[]{:S(2)}) copy-start(bf16[27,128,16]{1,2,0:T(8,128)(2,1)} %param.19) | copy-start | bytes 331780
  0.7 6.7 %copy-start.2 = (bf16[1,2,2,16,512]{4,3,2,1,0:T(8,128)(2,1)S(1)}, bf16[1,2,2,16,512]{4,3,2,1,0:T(8,128)(2,1)}, u32[]{:S(2)}) copy-start(bf16[1,2,2,16,512]{4,3,2,1,0:T(8,128)(2,1)} %param.15) | copy-start | bytes 196612
  3.4 17.1 %collective-permute-start.7 = (bf16[64,1920]{1,0:T(8,128)(2,1)}, bf16[64,1920]{1,0:T(8,128)(2,1)S(1)}, u32[]{:S(2)}, u32[]{:S(2)}) collective-permute-start(bf16[64,1920]{1,0:T(8,128)(2,1)} %get-tuple-element.22), channel_id=1, source_target_pairs={{0,5},{1,4},{2,7},{3,6},{4,1},{5,0},{6,3},{7,2},{8,13},{9,12},{10,... | collective-permute-start | bytes 737288 | tf_op jit(solution)/shard_map/weight_by_group/ppermute | solution.py:699
  7.4 5.6 %collective-permute-start = (bf16[64,512]{1,0:T(8,128)(2,1)S(1)}, bf16[64,512]{1,0:T(8,128)(2,1)S(1)}, u32[]{:S(2)}, u32[]{:S(2)}) collective-permute-start(bf16[64,512]{1,0:T(8,128)(2,1)S(1)} %bitcast.14), channel_id=1, source_target_pairs={{0,24},{2,0},{4,28},{6,4},{8,26},{10,2},{12,30},{14,6},{16,8},{18,... | collective-permute-start | bytes 196616 | tf_op jit(solution)/shard_map/gather_clips/ppermute | solution.py:711
  11.0 5.2 %collective-permute-start.1 = (bf16[64,512]{1,0:T(8,128)(2,1)S(1)}, bf16[64,512]{1,0:T(8,128)(2,1)S(1)}, u32[]{:S(2)}, u32[]{:S(2)}) collective-permute-start(bf16[64,512]{1,0:T(8,128)(2,1)S(1)} %bitcast.15), channel_id=1, source_target_pairs={{0,16},{2,24},{4,20},{6,28},{8,18},{10,26},{12,22},{14,30},{16,0},... | collective-permute-start | bytes 196616 | tf_op jit(solution)/shard_map/gather_clips/ppermute | solution.py:711
  11.0 10.7 %collective-permute-start.8 = (bf16[64,1920]{1,0:T(8,128)(2,1)}, bf16[64,1920]{1,0:T(8,128)(2,1)S(1)}, u32[]{:S(2)}, u32[]{:S(2)}) collective-permute-start(bf16[64,1920]{1,0:T(8,128)(2,1)} %get-tuple-element.23), channel_id=1, source_target_pairs={{0,4},{1,5},{2,6},{3,7},{4,0},{5,1},{6,2},{7,3},{8,12},{9,13},{10,... | collective-permute-start | bytes 737288 | tf_op jit(solution)/shard_map/weight_by_group/ppermute | solution.py:699
  11.5 10.2 %copy-start.1 = (bf16[64,2048]{1,0:T(8,128)(2,1)S(1)}, bf16[64,2048]{1,0:T(8,128)(2,1)}, u32[]{:S(2)}) copy-start(bf16[64,2048]{1,0:T(8,128)(2,1)} %get-tuple-element.21.own_ref) | copy-start | bytes 786436
  11.5 10.2 %collective-permute-start.9 = (bf16[64,1920]{1,0:T(8,128)(2,1)}, bf16[64,1920]{1,0:T(8,128)(2,1)S(1)}, u32[]{:S(2)}, u32[]{:S(2)}) collective-permute-start(bf16[64,1920]{1,0:T(8,128)(2,1)} %get-tuple-element.24), channel_id=1, source_target_pairs={{0,1},{1,0},{2,3},{3,2},{4,5},{5,4},{6,7},{7,6},{8,9},{9,8},{10,11... | collective-permute-start | bytes 737288 | tf_op jit(solution)/shard_map/weight_by_group/ppermute | solution.py:699
  13.0 5.0 %collective-permute-start.2 = (bf16[64,512]{1,0:T(8,128)(2,1)S(1)}, bf16[64,512]{1,0:T(8,128)(2,1)S(1)}, u32[]{:S(2)}, u32[]{:S(2)}) collective-permute-start(bf16[64,512]{1,0:T(8,128)(2,1)S(1)} %bitcast.16), channel_id=1, source_target_pairs={{0,8},{2,16},{4,12},{6,20},{8,10},{10,18},{12,14},{14,22},{16,24},... | collective-permute-start | bytes 196616 | tf_op jit(solution)/shard_map/gather_clips/ppermute | solution.py:711
  16.2 1.8 %collective-permute-start.3 = (bf16[64,512]{1,0:T(8,128)(2,1)S(1)}, bf16[64,512]{1,0:T(8,128)(2,1)S(1)}, u32[]{:S(2)}, u32[]{:S(2)}) collective-permute-start(bf16[64,512]{1,0:T(8,128)(2,1)S(1)} %bitcast.17), channel_id=1, source_target_pairs={{2,8},{6,12},{8,2},{12,6},{18,24},{22,28},{24,18},{28,22},{3,9},{7... | collective-permute-start | bytes 196616 | tf_op jit(solution)/shard_map/gather_clips/ppermute | solution.py:711
  18.0 6.0 %collective-permute-start.4 = (bf16[2,64,512]{2,1,0:T(8,128)(2,1)S(1)}, bf16[2,64,512]{2,1,0:T(8,128)(2,1)S(1)}, u32[]{:S(2)}, u32[]{:S(2)}) collective-permute-start(bf16[2,64,512]{2,1,0:T(8,128)(2,1)S(1)} %get-tuple-element.20), channel_id=1, source_target_pairs={{0,1},{1,0},{2,3},{3,2},{4,5},{5,4},{6,7},{7,6},{8,9},{9,8},{10,11... | collective-permute-start | bytes 393224 | tf_op jit(solution)/shard_map/spread_clips/ppermute | solution.py:726
  19.0 5.1 %collective-permute-start.5 = (bf16[2,64,512]{2,1,0:T(8,128)(2,1)S(1)}, bf16[2,64,512]{2,1,0:T(8,128)(2,1)S(1)}, u32[]{:S(2)}, u32[]{:S(2)}) collective-permute-start(bf16[2,64,512]{2,1,0:T(8,128)(2,1)S(1)} %get-tuple-element.19.refs_0_), channel_id=1, source_target_pairs={{0,4},{1,5},{2,6},{3,7},{4,0},{5,1},{6,2},{7,3},{8,12},{9,13},{10,... | collective-permute-start | bytes 393224 | tf_op jit(solution)/shard_map/spread_clips/ppermute | solution.py:726
  20.5 7.1 %collective-permute-start.6 = (bf16[2,64,512]{2,1,0:T(8,128)(2,1)S(1)}, bf16[2,64,512]{2,1,0:T(8,128)(2,1)S(1)}, u32[]{:S(2)}, u32[]{:S(2)}) collective-permute-start(bf16[2,64,512]{2,1,0:T(8,128)(2,1)S(1)} %get-tuple-element.20), channel_id=1, source_target_pairs={{0,5},{1,4},{2,7},{3,6},{4,1},{5,0},{6,3},{7,2},{8,13},{9,12},{10,... | collective-permute-start | bytes 393224 | tf_op jit(solution)/shard_map/spread_clips/ppermute | solution.py:726
  22.2 5.4 %copy-start.4 = (f32[64,2]{1,0:T(8,128)S(1)}, f32[64,2]{1,0:T(8,128)}, u32[]{:S(2)}) copy-start(f32[64,2]{1,0:T(8,128)} %get-tuple-element.25.scale_ref) | copy-start | bytes 1540
  22.2 5.4 %collective-permute-start.10 = (bf16[992,512]{1,0:T(8,128)(2,1)S(1)}, bf16[992,512]{1,0:T(8,128)(2,1)S(1)}, u32[]{:S(2)}, u32[]{:S(2)}) collective-permute-start(bf16[992,512]{1,0:T(8,128)(2,1)S(1)} %join_weights.1.wt_ref), channel_id=1, source_target_pairs={{0,2},{2,0},{4,6},{6,4},{1,3},{3,1},{5,7},{7,5},{8,10},{10,8},{12,... | collective-permute-start | bytes 3047432 | tf_op jit(solution)/shard_map/join_weights/ppermute | solution.py:743
  31.3 13.3 %all-to-all-start = ((f32[32,8,128]{2,1,0:T(8,128)}), f32[32,8,128]{2,1,0:T(8,128)S(1)}, u32[]{:S(2)}, u32[]{:S(2)}) async-start(f32[32,8,128]{2,1,0:T(8,128)} %convolutions.1), calls=%async_computation | async-start | bytes 262144 | tf_op jit(solution)/shard_map/sum_latents/all_to_all | solution.py:791
  35.9 8.2 %copy-start.3 = (f32[56,128]{1,0:T(8,128)S(1)}, f32[56,128]{1,0:T(8,128)}, u32[]{:S(2)}) copy-start(f32[56,128]{1,0:T(8,128)} %get-tuple-element.26.table_ref) | copy-start | bytes 86020
  35.9 4.2 %collective-permute-start.11 = (bf16[32,512]{1,0:T(8,128)(2,1)S(1)}, bf16[32,512]{1,0:T(8,128)(2,1)S(1)}, u32[]{:S(2)}, u32[]{:S(2)}) collective-permute-start(bf16[32,512]{1,0:T(8,128)(2,1)S(1)} %add_convert_fusion.m0_ref), channel_id=1, source_target_pairs={{0,1},{1,0},{2,3},{3,2},{4,5},{5,4},{6,7},{7,6},{8,9},{9,8},{10,11... | collective-permute-start | bytes 98312 | tf_op jit(solution)/shard_map/merged_projection/ppermute | solution.py:750
  37.8 4.1 %collective-permute-start.12 = (bf16[32,512]{1,0:T(8,128)(2,1)S(1)}, bf16[32,512]{1,0:T(8,128)(2,1)S(1)}, u32[]{:S(2)}, u32[]{:S(2)}) collective-permute-start(bf16[32,512]{1,0:T(8,128)(2,1)S(1)} %add_convert_fusion.m0_ref), channel_id=1, source_target_pairs={{0,4},{1,5},{2,6},{3,7},{4,0},{5,1},{6,2},{7,3},{8,12},{9,13},{10,... | collective-permute-start | bytes 98312 | tf_op jit(solution)/shard_map/merged_projection/ppermute | solution.py:750
  39.2 4.9 %collective-permute-start.13 = (bf16[32,512]{1,0:T(8,128)(2,1)S(1)}, bf16[32,512]{1,0:T(8,128)(2,1)S(1)}, u32[]{:S(2)}, u32[]{:S(2)}) collective-permute-start(bf16[32,512]{1,0:T(8,128)(2,1)S(1)} %add_convert_fusion.m0_ref), channel_id=1, source_target_pairs={{0,5},{1,4},{2,7},{3,6},{4,1},{5,0},{6,3},{7,2},{8,13},{9,12},{10,... | collective-permute-start | bytes 98312 | tf_op jit(solution)/shard_map/merged_projection/ppermute | solution.py:750
